TPU v7x, 32 devices: a whole 2x2x4 slice. The times are simulated.
32 devices in a mesh: dp: 4 (over y, x), ctx: 8 (over z, core).
Axes of the slice: x: 2, y: 2, z: 4, core: 2. Of those that a mesh axis runs over, the one named last changes fastest.
Arguments:
- queries: bfloat16 [8192, 512], P(('dp', 'ctx')), parts along dimension 0, may hold values from -60 to 60
- keys: bfloat16 [8192, 512], P(('dp', 'ctx')), parts along dimension 0, may hold values from -6 to 6
- values: bfloat16 [8192, 512], P(('dp', 'ctx')), parts along dimension 0, may hold values from -6 to 6
- grad_out: bfloat16 [8192, 512], P(('dp', 'ctx')), parts along dimension 0, may hold values from -6 to 6
- window: int32 [4], replicated, may hold values from 128 to 256, as said below
- offsets: int32 [128, 4], P(('dp', 'ctx')), parts along dimension 0, may hold values from 5 to 67, as said below
Outputs:
- attended: bfloat16 [8192, 512], P(('dp', 'ctx')), parts along dimension 0
- grad_queries: bfloat16 [8192, 512], P(('dp', 'ctx')), parts along dimension 0
- grad_keys: bfloat16 [8192, 512], P(('dp', 'ctx')), parts along dimension 0
- grad_values: bfloat16 [8192, 512], P(('dp', 'ctx')), parts along dimension 0
There are 4 independent parts, one for each index of `dp`. A program takes and returns all parts, laid end to end along the dimension named above; an argument that names none is the same for every part. Nothing has to cross between parts.
Inputs may be any that keep to these rules, and one draw needn't show every extreme that they name: `window`: every entry is between 128 and 256; some head has exactly 256 and some exactly 128. offsets[b, j] = 2 ** (j + 1) * 4 + (b % 4) - c with 0 <= c < 4, so the key block b - offsets[b, j] lies among the blocks of group b // 4 - 2 ** (j + 1).
All inputs are finite; a program needn't handle non-finite values.
Results may differ from a plain program's by a relative error of at most 0.017.
Values may be sent and summed in bfloat16 or wider, within the bound.
A program may use at most 64 MiB of HBM per device.

v0:
```python
import jax
import jax.numpy as jnp
from jax import lax
from jax.sharding import PartitionSpec as P

BLOCK = 64
LEVELS = 4


def passed_along(array, axis, by):
    size = lax.axis_size(axis)
    pairs = [(i, i + by) for i in range(size) if 0 <= i + by < size]
    return lax.ppermute(array, axis, pairs)


def as_sent(array):

    def short(part):
        return part.astype(jnp.bfloat16) if part.dtype == jnp.float32 else part

    return jax.tree.map(short, array)


def local_pass(
    rank_index,
    query_rows,
    key_prev,
    key_own,
    value_prev,
    value_own,
    level_kv,
    grad_rows,
    window,
    offset_rows,
):
    row_count, feat_count = query_rows.shape
    head_count = window.shape[0]
    head_size = feat_count // head_count
    block_count = row_count // BLOCK
    score_scale = head_size ** (-0.5)
    f32 = jnp.float32
    query_pos = rank_index * row_count + jnp.arange(row_count, dtype=jnp.int32)
    key_pos = rank_index * row_count - row_count + jnp.arange(2 * row_count, dtype=jnp.int32)
    query_heads = query_rows.reshape(row_count, head_count, head_size)
    query_blocks = query_rows.reshape(block_count, BLOCK, head_count, head_size)
    grad_heads = grad_rows.reshape(row_count, head_count, head_size)
    grad_blocks = grad_rows.reshape(block_count, BLOCK, head_count, head_size)
    win_keys = jnp.concatenate([key_prev, key_own], 0).reshape(2 * row_count, head_count, head_size)
    win_values = jnp.concatenate([value_prev, value_own], 0).reshape(
        2 * row_count, head_count, head_size
    )
    block_ids = rank_index * block_count + jnp.arange(block_count, dtype=jnp.int32)
    picked_keys = []
    picked_values = []
    level_ok = []
    block_index = []
    for depth_index in range(LEVELS):
        source = rank_index - 2 ** (depth_index + 1)
        inside = jnp.clip(
            block_ids - offset_rows[:, depth_index] - source * block_count, 0, block_count - 1
        )
        block_index.append(inside)
        far_keys, far_values = level_kv[depth_index]
        picked_keys.append(far_keys.reshape(block_count, BLOCK, feat_count)[inside])
        picked_values.append(far_values.reshape(block_count, BLOCK, feat_count)[inside])
        level_ok.append(jnp.broadcast_to(source >= 0, (BLOCK,)))
    log_width = LEVELS * BLOCK
    log_keys = jnp.stack(picked_keys, 1).reshape(block_count, log_width, head_count, head_size)
    log_values = jnp.stack(picked_values, 1).reshape(block_count, log_width, head_count, head_size)
    log_allowed = jnp.concatenate(level_ok, 0)
    win_scores = (
        jnp.einsum("qhd,khd->hqk", query_heads, win_keys, preferred_element_type=f32) * score_scale
    )
    log_scores = (
        jnp.einsum("pqhd,pkhd->hpqk", query_blocks, log_keys, preferred_element_type=f32).reshape(
            head_count, row_count, log_width
        )
        * score_scale
    )
    win_allowed = (
        (key_pos[None, None, :] <= query_pos[None, :, None])
        & (key_pos[None, None, :] > query_pos[None, :, None] - window[:, None, None])
        & (key_pos[None, None, :] >= 0)
    )
    allowed = jnp.concatenate(
        [
            win_allowed,
            jnp.broadcast_to(log_allowed[None, None, :], (head_count, row_count, log_width)),
        ],
        -1,
    )
    scores = jnp.where(allowed, jnp.concatenate([win_scores, log_scores], -1), f32(-1e30))
    top = jnp.max(scores, -1)
    weights = jnp.exp(scores - top[..., None])
    total = jnp.sum(weights, -1)
    weights_low = weights.astype(jnp.bfloat16)
    split_at = 2 * row_count
    out_win = jnp.einsum(
        "hqk,khd->qhd", weights_low[..., :split_at], win_values, preferred_element_type=f32
    )
    out_log = jnp.einsum(
        "hpqk,pkhd->pqhd",
        weights_low[..., split_at:].reshape(head_count, block_count, BLOCK, log_width),
        log_values,
        preferred_element_type=f32,
    ).reshape(row_count, head_count, head_size)
    attended = ((out_win + out_log) / total.T[:, :, None]).astype(jnp.bfloat16)
    lse = top + jnp.log(total)
    probs = jnp.exp(scores - lse[..., None])
    probs_low = probs.astype(jnp.bfloat16)
    delta = jnp.sum(grad_heads.astype(f32) * attended.astype(f32), -1).T
    dprob_win = jnp.einsum("qhd,khd->hqk", grad_heads, win_values, preferred_element_type=f32)
    dprob_log = jnp.einsum(
        "pqhd,pkhd->hpqk", grad_blocks, log_values, preferred_element_type=f32
    ).reshape(head_count, row_count, log_width)
    dscore = probs * (jnp.concatenate([dprob_win, dprob_log], -1) - delta[..., None])
    dscore_low = dscore.astype(jnp.bfloat16)
    dscore_win = dscore_low[..., :split_at]
    dscore_log = dscore_low[..., split_at:].reshape(head_count, block_count, BLOCK, log_width)
    probs_win = probs_low[..., :split_at]
    probs_log = probs_low[..., split_at:].reshape(head_count, block_count, BLOCK, log_width)
    grad_q = (
        jnp.einsum("hqk,khd->qhd", dscore_win, win_keys, preferred_element_type=f32)
        + jnp.einsum("hpqk,pkhd->pqhd", dscore_log, log_keys, preferred_element_type=f32).reshape(
            row_count, head_count, head_size
        )
    ) * score_scale
    grad_q = grad_q.astype(jnp.bfloat16).reshape(row_count, feat_count)
    dkey_win = (
        jnp.einsum("hqk,qhd->khd", dscore_win, query_heads, preferred_element_type=f32)
        * score_scale
    ).reshape(split_at, feat_count)
    dval_win = jnp.einsum(
        "hqk,qhd->khd", probs_win, grad_heads, preferred_element_type=f32
    ).reshape(split_at, feat_count)
    dkey_log = (
        jnp.einsum("hpqk,pqhd->pkhd", dscore_log, query_blocks, preferred_element_type=f32)
        * score_scale
    ).reshape(block_count, LEVELS, BLOCK, feat_count)
    dval_log = jnp.einsum(
        "hpqk,pqhd->pkhd", probs_log, grad_blocks, preferred_element_type=f32
    ).reshape(block_count, LEVELS, BLOCK, feat_count)
    level_parts = []
    for depth_index in range(LEVELS):
        onehot = (
            block_index[depth_index][:, None] == jnp.arange(block_count, dtype=jnp.int32)[None, :]
        ).astype(f32)
        part_key = (
            jnp.einsum(
                "pc,pkf->ckf", onehot, dkey_log[:, depth_index], precision=lax.Precision.HIGHEST
            )
            .reshape(row_count, feat_count)
            .astype(jnp.bfloat16)
        )
        part_value = (
            jnp.einsum(
                "pc,pkf->ckf", onehot, dval_log[:, depth_index], precision=lax.Precision.HIGHEST
            )
            .reshape(row_count, feat_count)
            .astype(jnp.bfloat16)
        )
        level_parts.append((part_key, part_value))
    prev_part = (
        dkey_win[:row_count].astype(jnp.bfloat16),
        dval_win[:row_count].astype(jnp.bfloat16),
    )
    return (
        attended.reshape(row_count, feat_count),
        grad_q,
        dkey_win[row_count:],
        dval_win[row_count:],
        prev_part,
        level_parts,
    )


def on_device(queries, keys, values, grad_out, window, offsets):
    rank_index = lax.axis_index("ctx")
    key_prev, value_prev = passed_along((keys, values), "ctx", 1)
    level_kv = []
    for depth_index in range(LEVELS):
        level_kv.append(passed_along((keys, values), "ctx", 2 ** (depth_index + 1)))
    attended, grad_q, own_dkey, own_dval, prev_part, level_parts = local_pass(
        rank_index, queries, key_prev, keys, value_prev, values, level_kv, grad_out, window, offsets
    )
    back_key, back_value = passed_along((prev_part[0], prev_part[1]), "ctx", -1)
    grad_keys = own_dkey + back_key.astype(jnp.float32)
    grad_values = own_dval + back_value.astype(jnp.float32)
    for depth_index in range(LEVELS):
        far_key, far_value = passed_along(
            as_sent(level_parts[depth_index]), "ctx", -(2 ** (depth_index + 1))
        )
        grad_keys = grad_keys + far_key.astype(jnp.float32)
        grad_values = grad_values + far_value.astype(jnp.float32)
    return (attended, grad_q, grad_keys.astype(jnp.bfloat16), grad_values.astype(jnp.bfloat16))


def solution(mesh):
    return jax.shard_map(
        on_device,
        mesh=mesh,
        in_specs=(
            P(("dp", "ctx"), None),
            P(("dp", "ctx"), None),
            P(("dp", "ctx"), None),
            P(("dp", "ctx"), None),
            P(),
            P(("dp", "ctx"), None),
        ),
        out_specs=(
            P(("dp", "ctx"), None),
            P(("dp", "ctx"), None),
            P(("dp", "ctx"), None),
            P(("dp", "ctx"), None),
        ),
        check_vma=False,
    )
```

profile of v0, /device:TPU:0, one launch (start us, length us, event | category | flops | bytes accessed | tf_op | source)
XLA Modules:
  0.0 154.6 jit_solution(17780732074131779874)
XLA Ops:
  0.7 5.1 %collective-permute-start.2 = (bf16[256,512]{1,0:T(8,128)(2,1)}, bf16[256,512]{1,0:T(8,128)(2,1)S(1)}, u32[]{:S(2)}, u32[]{:S(2)}) collective-permute-start(bf16[256,512]{1,0:T(8,128)(2,1)} %param.7), channel_id=1, source_target_pairs={{0,2},{1,3},{2,4},{3,5},{4,6},{5,7},{8,10},{9,11},{10,12},{11,13},... | collective-permute-start | bytes 786440 | tf_op jit(solution)/shard_map/ppermute | solution.py:13
  6.4 4.5 %collective-permute-start.3 = (bf16[256,512]{1,0:T(8,128)(2,1)}, bf16[256,512]{1,0:T(8,128)(2,1)S(1)}, u32[]{:S(2)}, u32[]{:S(2)}) collective-permute-start(bf16[256,512]{1,0:T(8,128)(2,1)} %param.7), channel_id=1, source_target_pairs={{0,4},{1,5},{2,6},{3,7},{8,12},{9,13},{10,14},{11,15},{16,20},{17,... | collective-permute-start | bytes 786440 | tf_op jit(solution)/shard_map/ppermute | solution.py:13
  10.9 1.3 collective-permute-start.5
  13.8 1.3 and_and_fusion
  15.1 1.1 fusion.53
  16.3 2.0 %collective-permute-start = (bf16[256,512]{1,0:T(8,128)(2,1)}, bf16[256,512]{1,0:T(8,128)(2,1)}, u32[]{:S(2)}, u32[]{:S(2)}) collective-permute-start(bf16[256,512]{1,0:T(8,128)(2,1)} %param.8), channel_id=1, source_target_pairs={{0,1},{1,2},{2,3},{3,4},{4,5},{5,6},{6,7},{8,9},{9,10},{10,11},{11... | collective-permute-start | bytes 786440 | tf_op jit(solution)/shard_map/ppermute | solution.py:13
  18.4 1.0 reshape.215
  19.4 1.8 %copy.55 = bf16[256,512]{0,1:T(8,128)(2,1)} copy(bf16[256,512]{1,0:T(8,128)(2,1)} %param.9) | data formatting | bytes 524288 | tf_op args[3]
  24.9 1.9 %collective-permute-start.6 = (bf16[256,512]{1,0:T(8,128)(2,1)}, bf16[256,512]{1,0:T(8,128)(2,1)S(1)}, u32[]{:S(2)}, u32[]{:S(2)}) collective-permute-start(bf16[256,512]{1,0:T(8,128)(2,1)} %param.8), channel_id=1, source_target_pairs={{0,4},{1,5},{2,6},{3,7},{8,12},{9,13},{10,14},{11,15},{16,20},{17,... | collective-permute-start | bytes 786440 | tf_op jit(solution)/shard_map/ppermute | solution.py:13
  26.7 1.3 gather_fusion.7
  28.0 1.3 gather_fusion.6
  29.3 2.6 %collective-permute-start.1 = (bf16[256,512]{0,1:T(8,128)(2,1)}, bf16[256,512]{0,1:T(8,128)(2,1)}, u32[]{:S(2)}, u32[]{:S(2)}) collective-permute-start(bf16[256,512]{0,1:T(8,128)(2,1)} %copy.42), channel_id=1, source_target_pairs={{0,1},{1,2},{2,3},{3,4},{4,5},{5,6},{6,7},{8,9},{9,10},{10,11},{11... | collective-permute-start | bytes 786440 | tf_op jit(solution)/shard_map/ppermute | solution.py:13
  33.5 1.3 gather_fusion.4
  34.8 1.1 pad_maximum_fusion.2
  35.9 1.0 copy.41
  37.5 1.1 pad_maximum_fusion.1
  39.4 1.3 copy.60
  40.7 1.4 convolution_multiply_fusion.1
  42.5 1.1 pad_maximum_fusion.3
  44.5 1.4 multiply_bitcast_fusion.1
  46.4 1.8 %fusion.2 = (f32[4,256]{1,0:T(4,128)S(1)}, bf16[4,256,768]{1,2,0:T(8,128)(2,1)S(1)}) fusion(f32[4,256]{1,0:T(4,128)S(1)} %fusion.57, f32[4,256,256]{1,2,0:T(8,128)S(1)} %copy.48, f32[4,256,512]{1,2,0:T(8,128)S(1)} %multiply_bitcast_fusion.1, pred[768]{0:T(1024)(128)(4,1)S(1)} %pad.15.clone, pred[4,256,512]{1,2,0:T(8,128)(4,1)S(1)} %copy-done.5), kind=kLoop, calls=%fused_computation.14 | loop fusion | flops 4717568 | bytes 5251840 | tf_op jit(solution)/shard_map/reduce_sum | solution.py:95
  48.2 1.1 copy-done.14
  50.2 2.0 %copy.50 = bf16[4,256,256]{2,1,0:T(8,128)(2,1)} copy(bf16[4,256,256]{1,2,0:T(8,128)(2,1)} %slice.117) | data formatting | bytes 1048576 | tf_op jit(solution)/shard_map/slice | solution.py:103
  52.2 1.7 %convolution_bitcast_fusion.4 = f32[4,64,4,128]{3,1,2,0:T(8,128)S(1)} fusion(bf16[4,256,4,128]{3,2,1,0:T(4,128)(2,1)} %copy-done.4, bf16[4,4,64,256]{3,2,1,0:T(8,128)(2,1)} %bitcast.151), kind=kOutput, calls=%fused_computation.27 | convolution fusion | flops 67108864 | bytes 2097152 | tf_op jit(solution)/shard_map/hpqk,pkhd->pqhd/dot_general | solution.py:101
  54.8 2.0 %copy.54 = f32[256,4,128]{0,2,1:T(8,128)} copy(f32[256,4,128]{2,0,1:T(8,128)} %bitcast.146) | data formatting | bytes 1048576 | tf_op jit(solution)/shard_map/reshape | solution.py:106
  56.8 1.7 %convolution_bitcast_fusion.1 = f32[4,256,512]{1,2,0:T(8,128)S(1)} fusion(bf16[512,4,128]{0,2,1:T(8,128)(2,1)} %bitcast.148, bf16[256,4,128]{0,2,1:T(8,128)(2,1)} %bitcast.143), kind=kOutput, calls=%fused_computation.21 | convolution fusion | flops 134217728 | bytes 2883584 | tf_op jit(solution)/shard_map/qhd,khd->hqk/dot_general | solution.py:112
  58.8 1.0 multiply_reduce_fusion
  60.3 2.1 %fusion.4 = (bf16[4,256,768]{1,2,0:T(8,128)(2,1)S(1)}, bf16[4,256,768]{1,2,0:T(8,128)(2,1)S(1)}) fusion(f32[4,256]{1,0:T(4,128)S(1)} %log_add_fusion, f32[4,256,256]{1,2,0:T(8,128)S(1)} %copy.48, f32[4,256,512]{1,2,0:T(8,128)S(1)} %multiply_bitcast_fusion.1, pred[768]{0:T(1024)(128)(4,1)S(1)} %pad.15.clone, pred[4,256,512]{1,2,0:T(8,128)(4,1)S(1)} %copy-done.6, ...), kind=kLoop, calls=%fused_computation.16 | loop fusion | flops 7077888 | bytes 9970432 | tf_op jit(solution)/shard_map/convert_element_type | solution.py:110
  63.3 1.4 convolution_bitcast_fusion.2
  64.8 1.5 fusion.5
  66.5 1.1 convolution_bitcast_fusion.3
  68.1 1.2 copy.85
  69.3 2.7 %copy.106 = f32[4,256,4,128]{3,2,0,1:T(4,128)} copy(f32[4,256,4,128]{3,1,2,0:T(8,128)S(1)} %multiply_bitcast_fusion) | data formatting | bytes 4194304 | tf_op jit(solution)/shard_map/reshape | solution.py:139
  72.0 2.6 %reshape.291 = f32[4,4,64,512]{3,0,2,1:T(4,128)S(1)} reshape(f32[4,256,4,128]{3,2,0,1:T(4,128)} %copy.106) | data formatting | bytes 4194304 | tf_op jit(solution)/shard_map/reshape | solution.py:139
  74.7 1.4 convolution_convert_fusion.4
  76.1 1.3 convolution_convert_fusion.5
  77.9 2.7 %copy.108 = f32[4,256,4,128]{3,2,0,1:T(4,128)} copy(f32[4,256,4,128]{3,1,2,0:T(8,128)S(1)} %convolution_bitcast_fusion) | data formatting | bytes 4194304 | tf_op jit(solution)/shard_map/reshape | solution.py:142
  80.6 3.4 %reshape.292 = f32[4,4,64,512]{3,0,2,1:T(4,128)} reshape(f32[4,256,4,128]{3,2,0,1:T(4,128)} %copy.108) | data formatting | bytes 4194304 | tf_op jit(solution)/shard_map/reshape | solution.py:142
  84.0 2.5 %convolution_convert_fusion = bf16[4,64,512]{2,0,1:T(4,128)(2,1)} fusion(f32[4,4,64,512]{3,0,2,1:T(4,128)} %reshape.292, s32[4]{0:T(128)S(1)} %get-tuple-element.17), kind=kOutput, calls=%fused_computation.36 | convolution fusion | flops 6422544 | bytes 786448 | tf_op jit(solution)/shard_map/pc,pkf->ckf/dot_general | solution.py:156
  86.5 2.3 %convolution_convert_fusion.1 = bf16[4,64,512]{2,0,1:T(4,128)(2,1)} fusion(f32[4,4,64,512]{3,0,2,1:T(4,128)} %reshape.292, s32[4]{0:T(128)S(1)} %get-tuple-element.18), kind=kOutput, calls=%fused_computation.37 | convolution fusion | flops 6422544 | bytes 786448 | tf_op jit(solution)/shard_map/pc,pkf->ckf/dot_general | solution.py:156
  88.8 2.0 %copy.65 = f32[4,64,4,128]{3,1,0,2:T(8,128)} copy(f32[4,64,4,128]{3,1,2,0:T(8,128)} %convolution_bitcast_fusion.3) | data formatting | bytes 1048576 | tf_op jit(solution)/shard_map/hpqk,pkhd->pqhd/transpose | solution.py:124
  90.8 2.0 %copy.66 = f32[256,4,128]{0,2,1:T(8,128)} copy(f32[256,4,128]{2,0,1:T(8,128)} %bitcast.147) | data formatting | bytes 1048576 | tf_op jit(solution)/shard_map/reshape | solution.py:124
  92.8 1.4 fusion.11
  95.0 1.9 %copy.69 = bf16[256,512]{1,0:T(8,128)(2,1)} copy(bf16[256,512]{0,1:T(8,128)(2,1)} %bitcast.158) | data formatting | bytes 524288 | tf_op jit(solution)/shard_map/convert_element_type | solution.py:164
  96.9 1.3 collective-permute-start.8
  98.2 1.7 %copy.81 = bf16[4,64,512]{2,1,0:T(8,128)(2,1)} copy(bf16[4,64,512]{2,0,1:T(4,128)(2,1)} %convolution_convert_fusion.4) | data formatting | bytes 524288 | tf_op jit(solution)/shard_map/convert_element_type | solution.py:153
  99.9 1.8 %copy.79 = bf16[4,64,512]{2,1,0:T(8,128)(2,1)} copy(bf16[4,64,512]{2,0,1:T(4,128)(2,1)} %convolution_convert_fusion.5) | data formatting | bytes 524288 | tf_op jit(solution)/shard_map/convert_element_type | solution.py:153
  101.7 1.6 %convolution_convert_fusion.6 = bf16[4,64,512]{2,0,1:T(4,128)(2,1)S(1)} fusion(f32[4,4,64,512]{3,0,2,1:T(4,128)} %copy-done.8, s32[4]{0:T(128)S(1)} %get-tuple-element.16), kind=kOutput, calls=%fused_computation.42 | convolution fusion | flops 6422544 | bytes 786448 | tf_op jit(solution)/shard_map/pc,pkf->ckf/dot_general | solution.py:149
  103.3 1.6 %convolution_convert_fusion.7 = bf16[4,64,512]{2,0,1:T(4,128)(2,1)S(1)} fusion(f32[4,4,64,512]{3,0,2,1:T(4,128)} %copy-done.8, s32[4]{0:T(128)S(1)} %get-tuple-element.12), kind=kOutput, calls=%fused_computation.43 | convolution fusion | flops 6422544 | bytes 786448 | tf_op jit(solution)/shard_map/pc,pkf->ckf/dot_general | solution.py:149
  106.5 1.3 collective-permute-start.10
  107.8 1.3 collective-permute-start.9
  109.1 1.4 collective-permute-start.11
  110.4 1.4 collective-permute-start.12
  111.8 1.3 convolution_convert_fusion.3
  114.7 1.9 %copy.97 = bf16[256,512]{1,0:T(8,128)(2,1)} copy(bf16[256,512]{0,1:T(8,128)(2,1)} %bitcast.171) | data formatting | bytes 524288
  116.5 1.2 copy.84
  117.8 1.8 %copy.83 = bf16[256,512]{1,0:T(8,128)(2,1)} copy(bf16[256,512]{0,1:T(8,128)(2,1)} %bitcast.157) | data formatting | bytes 524288 | tf_op jit(solution)/shard_map/convert_element_type | solution.py:165
  121.4 1.1 copy.96
  124.2 1.3 collective-permute-start.13
  125.5 4.3 %collective-permute-done.10 = bf16[256,512]{1,0:T(8,128)(2,1)} collective-permute-done((bf16[256,512]{1,0:T(8,128)(2,1)}, bf16[256,512]{1,0:T(8,128)(2,1)}, u32[]{:S(2)}, u32[]{:S(2)}) %collective-permute-start.10) | collective-permute-done | bytes 262176 | tf_op jit(solution)/shard_map/ppermute | solution.py:13
  129.9 1.3 collective-permute-start.15
  131.2 1.3 collective-permute-start.14
  133.9 2.2 %add_convert_fusion.1 = bf16[256,512]{1,0:T(8,128)(2,1)} fusion(bf16[256,512]{1,0:T(8,128)(2,1)} %collective-permute-done.12, bf16[256,512]{1,0:T(8,128)(2,1)} %collective-permute-done.11, bf16[256,512]{1,0:T(8,128)(2,1)} %collective-permute-done.10, bf16[256,512]{1,0:T(8,128)(2,1)} %collective-permute-done.9, f32[256,512]{1,0:T(8,128)S(1)} %copy-done.19, ...), kind=kLoop, calls=%fused_computation.70 | loop fusion | flops 1441792 | bytes 2097152 | tf_op jit(solution)/shard_map/convert_element_type | solution.py:195
  136.1 17.6 %collective-permute-done.15 = bf16[256,512]{1,0:T(8,128)(2,1)S(1)} collective-permute-done((bf16[256,512]{1,0:T(8,128)(2,1)S(1)}, bf16[256,512]{1,0:T(8,128)(2,1)S(1)}, u32[]{:S(2)}, u32[]{:S(2)}) %collective-permute-start.15) | collective-permute-done | bytes 262176 | tf_op jit(solution)/shard_map/ppermute | solution.py:13
  (125 shorter events, 24.5 us)
Async XLA Ops:
  0.6 20.6 %copy-start.26 = (bf16[256,512]{1,0:T(8,128)(2,1)S(1)}, bf16[256,512]{1,0:T(8,128)(2,1)}, u32[]{:S(2)}) copy-start(bf16[256,512]{1,0:T(8,128)(2,1)} %param.7) | copy-start | bytes 786436
  0.6 21.4 %copy-start.21 = (bf16[256,512]{1,0:T(8,128)(2,1)S(1)}, bf16[256,512]{1,0:T(8,128)(2,1)}, u32[]{:S(2)}) copy-start(bf16[256,512]{1,0:T(8,128)(2,1)} %param.6) | copy-start | bytes 786436
  0.7 28.6 %collective-permute-start.2 = (bf16[256,512]{1,0:T(8,128)(2,1)}, bf16[256,512]{1,0:T(8,128)(2,1)S(1)}, u32[]{:S(2)}, u32[]{:S(2)}) collective-permute-start(bf16[256,512]{1,0:T(8,128)(2,1)} %param.7), channel_id=1, source_target_pairs={{0,2},{1,3},{2,4},{3,5},{4,6},{5,7},{8,10},{9,11},{10,12},{11,13},... | collective-permute-start | bytes 786440 | tf_op jit(solution)/shard_map/ppermute | solution.py:13
  5.7 10.6 %collective-permute-start.4 = (bf16[256,512]{1,0:T(8,128)(2,1)}, bf16[256,512]{1,0:T(8,128)(2,1)S(1)}, u32[]{:S(2)}, u32[]{:S(2)}) collective-permute-start(bf16[256,512]{1,0:T(8,128)(2,1)} %param.7), channel_id=1, source_target_pairs={} | collective-permute-start | bytes 786440 | tf_op jit(solution)/shard_map/ppermute | solution.py:13
  6.4 26.1 %collective-permute-start.3 = (bf16[256,512]{1,0:T(8,128)(2,1)}, bf16[256,512]{1,0:T(8,128)(2,1)S(1)}, u32[]{:S(2)}, u32[]{:S(2)}) collective-permute-start(bf16[256,512]{1,0:T(8,128)(2,1)} %param.7), channel_id=1, source_target_pairs={{0,4},{1,5},{2,6},{3,7},{8,12},{9,13},{10,14},{11,15},{16,20},{17,... | collective-permute-start | bytes 786440 | tf_op jit(solution)/shard_map/ppermute | solution.py:13
  10.9 22.6 %collective-permute-start.5 = (bf16[256,512]{1,0:T(8,128)(2,1)}, bf16[256,512]{1,0:T(8,128)(2,1)S(1)}, u32[]{:S(2)}, u32[]{:S(2)}) collective-permute-start(bf16[256,512]{1,0:T(8,128)(2,1)} %param.8), channel_id=1, source_target_pairs={{0,2},{1,3},{2,4},{3,5},{4,6},{5,7},{8,10},{9,11},{10,12},{11,13},... | collective-permute-start | bytes 786440 | tf_op jit(solution)/shard_map/ppermute | solution.py:13
  12.2 12.6 %collective-permute-start.7 = (bf16[256,512]{1,0:T(8,128)(2,1)}, bf16[256,512]{1,0:T(8,128)(2,1)S(1)}, u32[]{:S(2)}, u32[]{:S(2)}) collective-permute-start(bf16[256,512]{1,0:T(8,128)(2,1)} %param.8), channel_id=1, source_target_pairs={} | collective-permute-start | bytes 786440 | tf_op jit(solution)/shard_map/ppermute | solution.py:13
  16.3 18.5 %collective-permute-start = (bf16[256,512]{1,0:T(8,128)(2,1)}, bf16[256,512]{1,0:T(8,128)(2,1)}, u32[]{:S(2)}, u32[]{:S(2)}) collective-permute-start(bf16[256,512]{1,0:T(8,128)(2,1)} %param.8), channel_id=1, source_target_pairs={{0,1},{1,2},{2,3},{3,4},{4,5},{5,6},{6,7},{8,9},{9,10},{10,11},{11... | collective-permute-start | bytes 786440 | tf_op jit(solution)/shard_map/ppermute | solution.py:13
  24.9 12.1 %collective-permute-start.6 = (bf16[256,512]{1,0:T(8,128)(2,1)}, bf16[256,512]{1,0:T(8,128)(2,1)S(1)}, u32[]{:S(2)}, u32[]{:S(2)}) collective-permute-start(bf16[256,512]{1,0:T(8,128)(2,1)} %param.8), channel_id=1, source_target_pairs={{0,4},{1,5},{2,6},{3,7},{8,12},{9,13},{10,14},{11,15},{16,20},{17,... | collective-permute-start | bytes 786440 | tf_op jit(solution)/shard_map/ppermute | solution.py:13
  29.3 13.2 %collective-permute-start.1 = (bf16[256,512]{0,1:T(8,128)(2,1)}, bf16[256,512]{0,1:T(8,128)(2,1)}, u32[]{:S(2)}, u32[]{:S(2)}) collective-permute-start(bf16[256,512]{0,1:T(8,128)(2,1)} %copy.42), channel_id=1, source_target_pairs={{0,1},{1,2},{2,3},{3,4},{4,5},{5,6},{6,7},{8,9},{9,10},{10,11},{11... | collective-permute-start | bytes 786440 | tf_op jit(solution)/shard_map/ppermute | solution.py:13
  33.5 7.2 %copy-start.2 = (bf16[4,256,4,128]{3,2,1,0:T(4,128)(2,1)}, bf16[4,256,4,128]{3,2,1,0:T(4,128)(2,1)S(1)}, u32[]{:S(2)}) copy-start(bf16[4,256,4,128]{3,2,1,0:T(4,128)(2,1)S(1)} %reshape.205) | copy-start | bytes 3145732
  33.5 4.0 %copy-start.23 = (bf16[4,64,512]{2,1,0:T(8,128)(2,1)S(1)}, bf16[4,64,512]{2,1,0:T(8,128)(2,1)}, u32[]{:S(2)}) copy-start(bf16[4,64,512]{2,1,0:T(8,128)(2,1)} %gather_fusion.7) | copy-start | bytes 786436
  33.5 4.0 %copy-start.24 = (bf16[4,64,512]{2,1,0:T(8,128)(2,1)S(1)}, bf16[4,64,512]{2,1,0:T(8,128)(2,1)}, u32[]{:S(2)}) copy-start(bf16[4,64,512]{2,1,0:T(8,128)(2,1)} %gather_fusion.6) | copy-start | bytes 786436
  38.9 1.8 %copy-start.4 = (bf16[4,256,4,128]{3,2,1,0:T(4,128)(2,1)}, bf16[4,256,4,128]{3,2,1,0:T(4,128)(2,1)S(1)}, u32[]{:S(2)}) copy-start(bf16[4,256,4,128]{3,2,1,0:T(4,128)(2,1)S(1)} %reshape.210) | copy-start | bytes 3145732
  42.5 3.4 %copy-start.5 = (pred[4,256,512]{1,2,0:T(8,128)(4,1)S(1)}, pred[4,256,512]{1,2,0:T(8,128)(4,1)}, u32[]{:S(2)}) copy-start(pred[4,256,512]{1,2,0:T(8,128)(4,1)} %and_and_fusion) | copy-start | bytes 1572868
  43.6 0.8 copy-start.9
  48.2 1.2 copy-start.14
  56.8 1.8 %copy-start.15 = (bf16[4,256,768]{1,2,0:T(8,128)(2,1)S(1)}, bf16[4,256,768]{1,2,0:T(8,128)(2,1)}, u32[]{:S(2)}) copy-start(bf16[4,256,768]{1,2,0:T(8,128)(2,1)} %copy-done.14) | copy-start | bytes 4718596
  56.8 1.8 %copy-start.18 = (bf16[256,512]{0,1:T(8,128)(2,1)S(1)}, bf16[256,512]{0,1:T(8,128)(2,1)}, u32[]{:S(2)}) copy-start(bf16[256,512]{0,1:T(8,128)(2,1)} %copy.55) | copy-start | bytes 786436
  56.8 1.8 %copy-start.20 = (bf16[512,512]{0,1:T(8,128)(2,1)S(1)}, bf16[512,512]{0,1:T(8,128)(2,1)}, u32[]{:S(2)}) copy-start(bf16[512,512]{0,1:T(8,128)(2,1)} %copy.41) | copy-start | bytes 1572868
  56.8 2.0 %copy-start.25 = (f32[256,4,128]{0,2,1:T(8,128)S(1)}, f32[256,4,128]{0,2,1:T(8,128)}, u32[]{:S(2)}) copy-start(f32[256,4,128]{0,2,1:T(8,128)} %copy.54) | copy-start | bytes 1572868
  58.8 1.0 copy-start.6
  58.8 1.5 copy-start.11
  62.4 2.3 %copy-start = (bf16[4,256,768]{1,2,0:T(8,128)(2,1)}, bf16[4,256,768]{1,2,0:T(8,128)(2,1)S(1)}, u32[]{:S(2)}) copy-start(bf16[4,256,768]{1,2,0:T(8,128)(2,1)S(1)} %get-tuple-element.21) | copy-start | bytes 4718596
  62.4 2.3 %copy-start.17 = (bf16[256,512]{0,1:T(8,128)(2,1)S(1)}, bf16[256,512]{0,1:T(8,128)(2,1)}, u32[]{:S(2)}) copy-start(bf16[256,512]{0,1:T(8,128)(2,1)} %copy.110) | copy-start | bytes 786436
  64.7 1.8 %copy-start.3 = (bf16[4,256,4,128]{3,2,1,0:T(4,128)(2,1)S(1)}, bf16[4,256,4,128]{3,2,1,0:T(4,128)(2,1)}, u32[]{:S(2)}) copy-start(bf16[4,256,4,128]{3,2,1,0:T(4,128)(2,1)} %copy-done.2) | copy-start | bytes 3145732
  66.3 1.3 copy-start.16
  74.7 3.2 %copy-start.8 = (f32[4,4,64,512]{3,0,2,1:T(4,128)}, f32[4,4,64,512]{3,0,2,1:T(4,128)S(1)}, u32[]{:S(2)}) copy-start(f32[4,4,64,512]{3,0,2,1:T(4,128)S(1)} %reshape.291) | copy-start | bytes 6291460
  84.0 8.9 %copy-start.1 = (bf16[4,256,768]{1,2,0:T(8,128)(2,1)S(1)}, bf16[4,256,768]{1,2,0:T(8,128)(2,1)}, u32[]{:S(2)}) copy-start(bf16[4,256,768]{1,2,0:T(8,128)(2,1)} %copy-done) | copy-start | bytes 4718596
  84.0 8.9 %copy-start.10 = (bf16[512,512]{0,1:T(8,128)(2,1)S(1)}, bf16[512,512]{0,1:T(8,128)(2,1)}, u32[]{:S(2)}) copy-start(bf16[512,512]{0,1:T(8,128)(2,1)} %copy-done.9) | copy-start | bytes 1572868
  88.8 5.4 %copy-start.13 = (f32[512,4,128]{0,2,1:T(8,128)S(1)}, f32[512,4,128]{0,2,1:T(8,128)}, u32[]{:S(2)}) copy-start(f32[512,4,128]{0,2,1:T(8,128)} %fusion.5) | copy-start | bytes 3145732
  95.0 16.9 %copy-start.7 = (f32[4,4,64,512]{3,0,2,1:T(4,128)S(1)}, f32[4,4,64,512]{3,0,2,1:T(4,128)}, u32[]{:S(2)}) copy-start(f32[4,4,64,512]{3,0,2,1:T(4,128)} %reshape.292) | copy-start | bytes 6291460
  96.9 27.3 %collective-permute-start.8 = (bf16[256,512]{1,0:T(8,128)(2,1)}, bf16[256,512]{1,0:T(8,128)(2,1)}, u32[]{:S(2)}, u32[]{:S(2)}) collective-permute-start(bf16[256,512]{1,0:T(8,128)(2,1)} %copy.69), channel_id=1, source_target_pairs={{1,0},{2,1},{3,2},{4,3},{5,4},{6,5},{7,6},{9,8},{10,9},{11,10},{12... | collective-permute-start | bytes 786440 | tf_op jit(solution)/shard_map/ppermute | solution.py:13
  99.9 13.2 %copy-start.12 = (f32[512,4,128]{0,2,1:T(8,128)S(1)}, f32[512,4,128]{0,2,1:T(8,128)}, u32[]{:S(2)}) copy-start(f32[512,4,128]{0,2,1:T(8,128)} %convolution_bitcast_fusion.2) | copy-start | bytes 3145732
  106.5 23.4 %collective-permute-start.10 = (bf16[256,512]{1,0:T(8,128)(2,1)}, bf16[256,512]{1,0:T(8,128)(2,1)}, u32[]{:S(2)}, u32[]{:S(2)}) collective-permute-start(bf16[256,512]{1,0:T(8,128)(2,1)} %bitcast.44), channel_id=1, source_target_pairs={{4,0},{5,1},{6,2},{7,3},{12,8},{13,9},{14,10},{15,11},{20,16},{21,... | collective-permute-start | bytes 786440 | tf_op jit(solution)/shard_map/ppermute | solution.py:13
  107.8 23.4 %collective-permute-start.9 = (bf16[256,512]{1,0:T(8,128)(2,1)}, bf16[256,512]{1,0:T(8,128)(2,1)}, u32[]{:S(2)}, u32[]{:S(2)}) collective-permute-start(bf16[256,512]{1,0:T(8,128)(2,1)} %bitcast.41), channel_id=1, source_target_pairs={{2,0},{3,1},{4,2},{5,3},{6,4},{7,5},{10,8},{11,9},{12,10},{13,11},... | collective-permute-start | bytes 786440 | tf_op jit(solution)/shard_map/ppermute | solution.py:13
  109.1 23.4 %collective-permute-start.11 = (bf16[256,512]{1,0:T(8,128)(2,1)}, bf16[256,512]{1,0:T(8,128)(2,1)}, u32[]{:S(2)}, u32[]{:S(2)}) collective-permute-start(bf16[256,512]{1,0:T(8,128)(2,1)} %bitcast.47), channel_id=1, source_target_pairs={} | collective-permute-start | bytes 786440 | tf_op jit(solution)/shard_map/ppermute | solution.py:13
  110.4 22.7 %collective-permute-start.12 = (bf16[256,512]{1,0:T(8,128)(2,1)}, bf16[256,512]{1,0:T(8,128)(2,1)}, u32[]{:S(2)}, u32[]{:S(2)}) collective-permute-start(bf16[256,512]{1,0:T(8,128)(2,1)} %bitcast.50), channel_id=1, source_target_pairs={} | collective-permute-start | bytes 786440 | tf_op jit(solution)/shard_map/ppermute | solution.py:13
  114.7 5.7 %slice-start = ((f32[512,4,128]{0,2,1:T(8,128)}), f32[256,4,128]{0,2,1:T(8,128)S(1)}, s32[]{:S(2)}) async-start(f32[512,4,128]{0,2,1:T(8,128)} %fusion.5), calls=%async_computation | async-start | bytes 1048576 | tf_op jit(solution)/shard_map/slice | solution.py:170
  120.4 3.1 %copy-start.22 = (bf16[4,64,512]{2,0,1:T(4,128)(2,1)S(1)}, bf16[4,64,512]{2,0,1:T(4,128)(2,1)}, u32[]{:S(2)}) copy-start(bf16[4,64,512]{2,0,1:T(4,128)(2,1)} %convolution_convert_fusion.3) | copy-start | bytes 786436
  121.4 2.8 %copy-start.27 = (bf16[256,512]{1,0:T(8,128)(2,1)S(1)}, bf16[256,512]{1,0:T(8,128)(2,1)}, u32[]{:S(2)}) copy-start(bf16[256,512]{1,0:T(8,128)(2,1)} %copy.83) | copy-start | bytes 786436
  121.4 12.4 %copy-start.19 = (f32[256,512]{1,0:T(8,128)S(1)}, f32[256,512]{1,0:T(8,128)}, u32[]{:S(2)}) copy-start(f32[256,512]{1,0:T(8,128)} %copy.70) | copy-start | bytes 1572868
  124.2 11.8 %collective-permute-start.13 = (bf16[256,512]{1,0:T(8,128)(2,1)S(1)}, bf16[256,512]{1,0:T(8,128)(2,1)S(1)}, u32[]{:S(2)}, u32[]{:S(2)}) collective-permute-start(bf16[256,512]{1,0:T(8,128)(2,1)S(1)} %copy-done.27), channel_id=1, source_target_pairs={{1,0},{2,1},{3,2},{4,3},{5,4},{6,5},{7,6},{9,8},{10,9},{11,10},{12... | collective-permute-start | bytes 786440 | tf_op jit(solution)/shard_map/ppermute | solution.py:13
  129.9 23.8 %collective-permute-start.15 = (bf16[256,512]{1,0:T(8,128)(2,1)S(1)}, bf16[256,512]{1,0:T(8,128)(2,1)S(1)}, u32[]{:S(2)}, u32[]{:S(2)}) collective-permute-start(bf16[256,512]{1,0:T(8,128)(2,1)S(1)} %bitcast.175), channel_id=1, source_target_pairs={{4,0},{5,1},{6,2},{7,3},{12,8},{13,9},{14,10},{15,11},{20,16},{21,... | collective-permute-start | bytes 786440 | tf_op jit(solution)/shard_map/ppermute | solution.py:13
  131.2 22.5 %collective-permute-start.14 = (bf16[256,512]{1,0:T(8,128)(2,1)S(1)}, bf16[256,512]{1,0:T(8,128)(2,1)S(1)}, u32[]{:S(2)}, u32[]{:S(2)}) collective-permute-start(bf16[256,512]{1,0:T(8,128)(2,1)S(1)} %bitcast.174), channel_id=1, source_target_pairs={{2,0},{3,1},{4,2},{5,3},{6,4},{7,5},{10,8},{11,9},{12,10},{13,11},... | collective-permute-start | bytes 786440 | tf_op jit(solution)/shard_map/ppermute | solution.py:13
  132.5 21.2 %collective-permute-start.16 = (bf16[256,512]{1,0:T(8,128)(2,1)S(1)}, bf16[256,512]{1,0:T(8,128)(2,1)S(1)}, u32[]{:S(2)}, u32[]{:S(2)}) collective-permute-start(bf16[256,512]{1,0:T(8,128)(2,1)S(1)} %bitcast.173), channel_id=1, source_target_pairs={} | collective-permute-start | bytes 786440 | tf_op jit(solution)/shard_map/ppermute | solution.py:13
  133.2 20.5 %collective-permute-start.17 = (bf16[256,512]{1,0:T(8,128)(2,1)S(1)}, bf16[256,512]{1,0:T(8,128)(2,1)S(1)}, u32[]{:S(2)}, u32[]{:S(2)}) collective-permute-start(bf16[256,512]{1,0:T(8,128)(2,1)S(1)} %bitcast.172), channel_id=1, source_target_pairs={} | collective-permute-start | bytes 786440 | tf_op jit(solution)/shard_map/ppermute | solution.py:13
where the time goes:
time: 158 us; the launch traced here: 155 us
  local copies, waits for them, and re-layouts  59.5 us (38%)
  starting transfers between devices  30.5 us (19%)
  matrix products  26.9 us (17%)
  waiting for transfers between devices  22 us (14%)
  other arithmetic  14.3 us (9%)
    ppermute x18, starting transfers between devices, passed_along(): return lax.ppermute(array, axis, pairs)  30.5 us
    ppermute x18, waiting for transfers between devices, passed_along(): return lax.ppermute(array, axis, pairs)  22 us
    unnamed x60, local copies, waits for them, and re-layouts  8.04 us
    dot_general x4, matrix products, local_pass(): jnp.einsum('pc,pkf->ckf', onehot, dval_log[:, depth_index], precision=lax...  6.71 us
    reshape x2, local copies, waits for them, and re-layouts, local_pass(): dval_log = jnp.einsum('hpqk,pqhd->pkhd', probs_log, grad_blocks, preferre...  6.12 us
    dot_general x4, matrix products, local_pass(): jnp.einsum('pc,pkf->ckf', onehot, dkey_log[:, depth_index], precision=lax...  5.94 us
    reshape x2, local copies, waits for them, and re-layouts, local_pass(): dkey_log = (jnp.einsum('hpqk,pqhd->pkhd', dscore_log, query_blocks, prefe...  5.32 us
    convert_element_type x4, local copies, waits for them, and re-layouts, local_pass(): part_key = jnp.einsum('pc,pkf->ckf', onehot, dkey_log[:, depth_index], pr...  5.02 us
  transfers between devices with their start and end apart: 18, of which 2 were waited for; matrix products, arithmetic and copies ran while one was open for 29% of the time, Pallas kernels for 0%

commit v1 on v0

v1 whole, which is shorter than its diff:
```python
import functools
import math

import jax
import jax.numpy as jnp
from jax import lax
from jax.experimental import pallas as pl
from jax.experimental.pallas import tpu as pltpu
from jax.sharding import PartitionSpec as P

BLOCK = 64
LEVELS = 4
HEAD = 128
NEG = -1e30
MESH = pl.DeviceIdType.MESH
NT = (((1,), (1,)), ((), ()))
TN = (((0,), (0,)), ((), ()))
NN = (((1,), (0,)), ((), ()))


def dot(a, b, dims):
    return lax.dot_general(a, b, dims, preferred_element_type=jnp.float32)


def kernel(
    size, heads, far,
    window, offsets, q_ref, k_ref, v_ref, do_ref,
    att_ref, gq_ref, gk_ref, gv_ref,
    own, rx1, rx2, rx4, rxf,
    tg1, tg4, ts2, tgf, rg1, rg4, rs2, rgf, hold2, acc,
    send, recv,
):
    f32, bf16 = jnp.float32, jnp.bfloat16
    rows = q_ref.shape[0]
    r = lax.axis_index("ctx")
    odd = lax.rem(r, 2) == 1
    even = jnp.logical_not(odd)
    has_up = r + 2 < size
    scale = HEAD ** -0.5
    mate = r + 1 - 2 * lax.rem(r, 2)

    K_OWN, K_REL, K_PRV, K_G4, K_S2, K_G1, K_FAR = 0, 1, 2, 3, 4, 5, 6
    K_GFAR = K_FAR + len(far)

    def copy(kind, h, src, dst, to):
        return pltpu.make_async_remote_copy(
            src_ref=src, dst_ref=dst, send_sem=send.at[kind, h], recv_sem=recv.at[kind, h],
            device_id={"ctx": to}, device_id_type=MESH,
        )

    def own_up(h):
        return copy(K_OWN, h, own.at[h], rx2.at[h], r + 2)

    def relay_up(h):
        return copy(K_REL, h, rx2.at[h], rx4.at[h], r + 2)

    def prev_own(h):
        return copy(K_PRV, h, own.at[h], rx1.at[h], mate)

    def prev_relay(h):
        return copy(K_PRV, h, rx2.at[h], rx1.at[h], mate)

    def far_up(n, h):
        return copy(K_FAR + n, h, own.at[h], rxf.at[n, h], r + far[n])

    def g4_down(h):
        return copy(K_G4, h, tg4.at[h], rg4.at[h], r - 2)

    def s2_down(h):
        return copy(K_S2, h, ts2.at[h], rs2.at[h], r - 2)

    def g1_mate(h):
        return copy(K_G1, h, tg1.at[h], rg1.at[h], mate)

    def gfar_down(n, h):
        return copy(K_GFAR + n, h, tgf.at[n, h], rgf.at[n, h], r - far[n])

    barrier = pltpu.get_barrier_semaphore()
    pl.semaphore_signal(barrier, inc=1, device_id={"ctx": mate}, device_id_type=MESH)
    count = 1
    for d in (2,) + far:
        for to, ok in ((r + d, r + d < size), (r - d, r >= d)):
            count = count + ok.astype(jnp.int32)

            @pl.when(ok)
            def _(to=to):
                pl.semaphore_signal(barrier, inc=1, device_id={"ctx": to}, device_id_type=MESH)

    for h in range(heads):
        cols = slice(h * HEAD, (h + 1) * HEAD)
        own[h, 0] = k_ref[:, cols]
        own[h, 1] = v_ref[:, cols]
    for d, buf in ((1, rx1), (2, rx2), (4, rx4)):

        @pl.when(r < d)
        def _(buf=buf):
            buf[...] = jnp.zeros_like(buf)

    for n, d in enumerate(far):

        @pl.when(r < d)
        def _(n=n):
            rxf[n] = jnp.zeros(rxf.shape[1:], bf16)

    pl.semaphore_wait(barrier, count)

    def start_own(h):
        @pl.when(has_up)
        def _():
            own_up(h).start()

        for n in range(len(far)):

            @pl.when(r + far[n] < size)
            def _(n=n):
                far_up(n, h).start()

    start_own(0)
    start_own(1)

    @pl.when(even)
    def _():
        for h in range(heads):
            prev_own(h).start()

    key_i = lax.broadcasted_iota(jnp.int32, (rows, rows), 0)
    query_i = lax.broadcasted_iota(jnp.int32, (rows, rows), 1)
    diff = key_i - query_i
    tri = diff <= 0
    key_block = key_i // BLOCK
    query_block = lax.broadcasted_iota(jnp.int32, (1, rows), 1) // BLOCK
    dists = (2, 4) + far
    picks = []
    for j, d in enumerate(dists):
        pick = jnp.zeros((1, rows), jnp.int32)
        for p in range(rows // BLOCK):
            inside = p + d * (rows // BLOCK) - offsets[p, j]
            pick = jnp.where(query_block == p, inside, pick)
        picks.append(jnp.where(r >= d, pick, -1))

    def compute(h):
        cols = slice(h * HEAD, (h + 1) * HEAD)
        q = q_ref[:, cols]
        do = do_ref[:, cols]
        sources = [own[h], rx1[h], rx2[h], rx4[h]] + [rxf[n, h] for n in range(len(far))]
        ks = [x[0] for x in sources]
        vs = [x[1] for x in sources]
        w = window[h]
        limit = jnp.where(r >= 1, rows - w, 2 * rows)
        ok_win = (tri & (diff > -w)) | (diff > limit)
        raw = [dot(k, q, NT) for k in ks]
        scores = [jnp.where(ok_win, jnp.where(tri, raw[0], raw[1]), NEG)]
        for pick, s in zip(picks, raw[2:]):
            scores.append(jnp.where(key_block == pick, s, NEG))
        top = functools.reduce(jnp.maximum, [jnp.max(s, 0, keepdims=True) for s in scores])
        c = scale * math.log2(math.e)
        weights = [jnp.exp2((s - top) * c) for s in scores]
        total = functools.reduce(jnp.add, [jnp.sum(x, 0, keepdims=True) for x in weights])
        inv = 1.0 / total
        probs = [x * inv for x in weights]

        def spread(parts):
            first = parts[0]
            cut = [jnp.where(tri, first, 0.0), jnp.where(tri, 0.0, first)] + parts[1:]
            return [x.astype(bf16) for x in cut]

        p_low = spread(probs)
        v_all = jnp.concatenate(vs, 0)
        out_t = dot(v_all, jnp.concatenate(p_low, 0), TN)
        att = out_t.T.astype(bf16)
        att_ref[:, cols] = att
        delta = jnp.sum((att.astype(f32) * do.astype(f32)).T, 0, keepdims=True)
        raw = [dot(v, do, NT) for v in vs]
        dprobs = [jnp.where(tri, raw[0], raw[1])] + raw[2:]
        ds = spread([p * (x - delta) for p, x in zip(probs, dprobs)])
        gq = dot(jnp.concatenate(ks, 0), jnp.concatenate(ds, 0), TN) * scale
        gq_ref[:, cols] = gq.T.astype(bf16)
        dk = [dot(x, q, NN) * scale for x in ds]
        dv = [dot(x, do, NN) for x in p_low]
        acc[h, 0] = dk[0]
        acc[h, 1] = dv[0]
        tg1[h, 0] = dk[1].astype(bf16)
        tg1[h, 1] = dv[1].astype(bf16)
        hold2[h, 0] = dk[2]
        hold2[h, 1] = dv[2]
        tg4[h, 0] = dk[3].astype(bf16)
        tg4[h, 1] = dv[3].astype(bf16)
        for n in range(len(far)):
            tgf[n, h, 0] = dk[4 + n].astype(bf16)
            tgf[n, h, 1] = dv[4 + n].astype(bf16)

        @pl.when(r >= 4)
        def _():
            g4_down(h).start()

        @pl.when(r >= 1)
        def _():
            g1_mate(h).start()

        for n in range(len(far)):

            @pl.when(r >= far[n])
            def _(n=n):
                gfar_down(n, h).start()

    def combine(h):
        @pl.when((r >= 2) & has_up)
        def _():
            g4_down(h).wait_recv()
            hold2[h] = hold2[h] + rg4[h].astype(f32)

        @pl.when(odd & (r >= 3))
        def _():
            g1_mate(h).wait_recv()
            hold2[h] = hold2[h] + rg1[h].astype(f32)

        @pl.when(r >= 2)
        def _():
            ts2[h] = hold2[h].astype(bf16)
            s2_down(h).start()

    for i in range(heads + 1):
        if i < heads:

            @pl.when(r >= 2)
            def _(i=i):
                own_up(i).wait_recv()

            @pl.when((r >= 2) & has_up)
            def _(i=i):
                relay_up(i).start()

            @pl.when(odd & (r >= 3))
            def _(i=i):
                prev_relay(i).start()

            if i + 2 < heads:
                start_own(i + 2)
        if i >= 1:
            h = i - 1

            @pl.when(r >= 1)
            def _(h=h):
                prev_own(h).wait_recv()

            @pl.when(r >= 4)
            def _(h=h):
                relay_up(h).wait_recv()

            for n in range(len(far)):

                @pl.when(r >= far[n])
                def _(n=n, h=h):
                    far_up(n, h).wait_recv()

            compute(h)
        if i >= 2:
            combine(i - 2)
    combine(heads - 1)

    for h in range(heads):
        cols = slice(h * HEAD, (h + 1) * HEAD)

        @pl.when(even)
        def _(h=h):
            g1_mate(h).wait_recv()
            acc[h] = acc[h] + rg1[h].astype(f32)

        for n in range(len(far)):

            @pl.when(r + far[n] < size)
            def _(n=n, h=h):
                gfar_down(n, h).wait_recv()
                acc[h] = acc[h] + rgf[n, h].astype(f32)

        @pl.when(has_up)
        def _(h=h):
            s2_down(h).wait_recv()
            acc[h] = acc[h] + rs2[h].astype(f32)

        gk_ref[:, cols] = acc[h, 0].astype(bf16)
        gv_ref[:, cols] = acc[h, 1].astype(bf16)

    for h in range(heads):

        @pl.when(has_up)
        def _(h=h):
            own_up(h).wait_send()

        @pl.when((r >= 2) & has_up)
        def _(h=h):
            relay_up(h).wait_send()

        @pl.when(even | (r >= 3))
        def _(h=h):
            prev_own(h).wait_send()

        @pl.when(r >= 4)
        def _(h=h):
            g4_down(h).wait_send()

        @pl.when(r >= 2)
        def _(h=h):
            s2_down(h).wait_send()

        @pl.when(r >= 1)
        def _(h=h):
            g1_mate(h).wait_send()

        for n in range(len(far)):

            @pl.when(r + far[n] < size)
            def _(n=n, h=h):
                far_up(n, h).wait_send()

            @pl.when(r >= far[n])
            def _(n=n, h=h):
                gfar_down(n, h).wait_send()


def on_device(queries, keys, values, grad_out, window, offsets):
    size = lax.axis_size("ctx")
    rows, feat = queries.shape
    heads = feat // HEAD
    far = tuple(2 ** (j + 1) for j in range(2, LEVELS) if 2 ** (j + 1) < size)
    nf = max(len(far), 1)
    kinds = 6 + 2 * len(far)
    vmem = pl.BlockSpec(memory_space=pltpu.VMEM)
    smem = pl.BlockSpec(memory_space=pltpu.SMEM)
    pack = (heads, 2, rows, HEAD)
    small = pltpu.VMEM(pack, jnp.bfloat16)
    wide = pltpu.VMEM(pack, jnp.float32)
    more = pltpu.VMEM((nf,) + (pack if far else (1, 2, 16, HEAD)), jnp.bfloat16)
    out = jax.ShapeDtypeStruct((rows, feat), jnp.bfloat16)
    return pl.pallas_call(
        functools.partial(kernel, size, heads, far),
        out_shape=(out,) * 4,
        in_specs=[smem, smem] + [vmem] * 4,
        out_specs=(vmem,) * 4,
        scratch_shapes=[small] * 4 + [more] + [small] * 3 + [more] + [small] * 3 + [more]
        + [wide] * 2
        + [pltpu.SemaphoreType.DMA((kinds, heads)), pltpu.SemaphoreType.DMA((kinds, heads))],
        compiler_params=pltpu.CompilerParams(
            collective_id=0, has_side_effects=True, vmem_limit_bytes=48 * 2**20
        ),
        cost_estimate=pl.CostEstimate(
            flops=12 * heads * rows * rows * HEAD * (4 + len(far)),
            bytes_accessed=16 * rows * feat,
            transcendentals=heads * rows * rows * (3 + len(far)),
        ),
    )(window, offsets, queries, keys, values, grad_out)


def solution(mesh):
    cut = P(("dp", "ctx"), None)
    return jax.shard_map(
        on_device,
        mesh=mesh,
        in_specs=(cut, cut, cut, cut, P(), cut),
        out_specs=(cut,) * 4,
        check_vma=False,
    )
```

time: 158 us -> 52.2 us (0.33); the launches traced: 155 us -> 52 us
  local copies, waits for them, and re-layouts: 59.5 us -> 7.94 us
  Pallas kernels: 0 us -> 43.4 us
  starting transfers between devices: 30.5 us -> 0 us
  matrix products: 26.9 us -> 0 us
  waiting for transfers between devices: 22 us -> 0 us
  other arithmetic: 14.3 us -> 0 us
    pallas_call x0 -> x1, Pallas kernels: none -> 43.4 us  [on_device(): pl.pallas_call(functools.partial(kernel, size, heads, far), out_shape=(ou...]
    ppermute x18 -> x0, starting transfers between devices: 30.5 us -> none  [passed_along(): return lax.ppermute(array, axis, pairs)]
    dot_general x20 -> x0, matrix products: 26.9 us -> none  [the longest x4 6.71 us: local_pass(): jnp.einsum('pc,pkf->ckf', onehot, dval_log[:, depth_index], precision=lax...]
    ppermute x18 -> x0, waiting for transfers between devices: 22 us -> none  [passed_along(): return lax.ppermute(array, axis, pairs)]
    reshape x12 -> x0, local copies, waits for them, and re-layouts: 20 us -> none  [the longest x2 6.12 us: local_pass(): dval_log = jnp.einsum('hpqk,pqhd->pkhd', probs_log, grad_blocks, preferre...]
    convert_element_type x10 -> x0, local copies, waits for them, and re-layouts: 10.9 us -> none  [the longest x4 5.02 us: local_pass(): part_key = jnp.einsum('pc,pkf->ckf', onehot, dkey_log[:, depth_index], pr...]
    slice x13 -> x0, local copies, waits for them, and re-layouts: 9.72 us -> none  [the longest x2 2.88 us: local_pass(): weights_low[..., split_at:]]
    gather x8 -> x0, local copies, waits for them, and re-layouts: 6.62 us -> none  [the longest x4 4.37 us: local_pass(): far_values.reshape(block_count, BLOCK, feat_count)[inside]]
  transfers between devices with their start and end apart: 18 -> 0, of which waited for: 2 -> 0; matrix products, arithmetic and copies ran while one was open for 29% -> 0% of each run, Pallas kernels for 0% -> 0%
where the time goes in v1:
time: 52.2 us; the launch traced here: 52 us
  Pallas kernels  43.4 us (83%)
  local copies, waits for them, and re-layouts  7.94 us (15%)
  between operations  0.66 us (1%)
    pallas_call x1, Pallas kernels, on_device(): pl.pallas_call(functools.partial(kernel, size, heads, far), out_shape=(ou...  43.4 us
    unnamed x16, local copies, waits for them, and re-layouts  7.94 us

profile of v1, /device:TPU:0, one launch (start us, length us, event | category | flops | bytes accessed | tf_op | source)
XLA Modules:
  0.0 52.0 jit_solution(15311027165682183549)
XLA Ops:
  0.6 0.0 copy-start
  0.6 0.9 %copy-done = bf16[256,512]{1,0:T(8,128)(2,1)S(1)} copy-done((bf16[256,512]{1,0:T(8,128)(2,1)S(1)}, bf16[256,512]{1,0:T(8,128)(2,1)}, u32[]{:S(2)}) %copy-start) | copy-done | bytes 262168
  1.6 0.0 copy-start.1
  1.6 0.9 %copy-done.1 = bf16[256,512]{1,0:T(8,128)(2,1)S(1)} copy-done((bf16[256,512]{1,0:T(8,128)(2,1)S(1)}, bf16[256,512]{1,0:T(8,128)(2,1)}, u32[]{:S(2)}) %copy-start.1) | copy-done | bytes 262168
  2.5 0.0 copy-start.2
  2.5 0.9 %copy-done.2 = bf16[256,512]{1,0:T(8,128)(2,1)S(1)} copy-done((bf16[256,512]{1,0:T(8,128)(2,1)S(1)}, bf16[256,512]{1,0:T(8,128)(2,1)}, u32[]{:S(2)}) %copy-start.2) | copy-done | bytes 262168
  3.5 0.0 copy-start.3
  3.5 0.9 %copy-done.3 = bf16[256,512]{1,0:T(8,128)(2,1)S(1)} copy-done((bf16[256,512]{1,0:T(8,128)(2,1)S(1)}, bf16[256,512]{1,0:T(8,128)(2,1)}, u32[]{:S(2)}) %copy-start.3) | copy-done | bytes 262168
  4.4 0.0 copy-start.4
  4.4 0.7 %copy-done.4 = s32[4,4]{1,0:T(4,128)S(1)} copy-done((s32[4,4]{1,0:T(4,128)S(1)}, s32[4,4]{1,0:T(4,128)}, u32[]{:S(2)}) %copy-start.4) | copy-done | bytes 88
  5.1 0.0 copy-start.5
  5.1 0.7 %copy-done.5 = s32[4]{0:T(128)S(1)} copy-done((s32[4]{0:T(128)S(1)}, s32[4]{0:T(128)}, u32[]{:S(2)}) %copy-start.5) | copy-done | bytes 40
  5.8 43.4 %shard_map.93 = (bf16[256,512]{1,0:T(8,128)(2,1)S(1)}, bf16[256,512]{1,0:T(8,128)(2,1)S(1)}, bf16[256,512]{1,0:T(8,128)(2,1)S(1)}, bf16[256,512]{1,0:T(8,128)(2,1)S(1)}) custom-call(s32[4]{0:T(128)S(1)} %copy-done.5, s32[4,4]{1,0:T(4,128)S(1)} %copy-done.4, bf16[256,512]{1,0:T(8,128)(2,1)S(1)} %copy-done, bf16[256,512]{1,0:T(8,128)(2,1)S(1)} %copy-done.1, ...), custom_call_target="tpu_custom_call" | custom-call | flops 1610612736 | bytes 2097152 | tf_op jit(solution)/shard_map/pallas_call | solution.py:335
  49.2 0.7 %copy.14 = bf16[256,512]{1,0:T(8,128)(2,1)} copy(bf16[256,512]{1,0:T(8,128)(2,1)S(1)} %get-tuple-element.8) | data formatting | bytes 524288
  49.9 0.7 %copy.15 = bf16[256,512]{1,0:T(8,128)(2,1)} copy(bf16[256,512]{1,0:T(8,128)(2,1)S(1)} %get-tuple-element.9) | data formatting | bytes 524288
  50.6 0.7 %copy.16 = bf16[256,512]{1,0:T(8,128)(2,1)} copy(bf16[256,512]{1,0:T(8,128)(2,1)S(1)} %get-tuple-element.10) | data formatting | bytes 524288
  51.3 0.7 %copy.17 = bf16[256,512]{1,0:T(8,128)(2,1)} copy(bf16[256,512]{1,0:T(8,128)(2,1)S(1)} %get-tuple-element.11) | data formatting | bytes 524288
Async XLA Ops:
  0.6 1.0 %copy-start = (bf16[256,512]{1,0:T(8,128)(2,1)S(1)}, bf16[256,512]{1,0:T(8,128)(2,1)}, u32[]{:S(2)}) copy-start(bf16[256,512]{1,0:T(8,128)(2,1)} %q_ref.1) | copy-start | bytes 786436
  1.6 0.9 %copy-start.1 = (bf16[256,512]{1,0:T(8,128)(2,1)S(1)}, bf16[256,512]{1,0:T(8,128)(2,1)}, u32[]{:S(2)}) copy-start(bf16[256,512]{1,0:T(8,128)(2,1)} %k_ref.1) | copy-start | bytes 786436
  2.5 0.9 %copy-start.2 = (bf16[256,512]{1,0:T(8,128)(2,1)S(1)}, bf16[256,512]{1,0:T(8,128)(2,1)}, u32[]{:S(2)}) copy-start(bf16[256,512]{1,0:T(8,128)(2,1)} %v_ref.1) | copy-start | bytes 786436
  3.5 0.9 %copy-start.3 = (bf16[256,512]{1,0:T(8,128)(2,1)S(1)}, bf16[256,512]{1,0:T(8,128)(2,1)}, u32[]{:S(2)}) copy-start(bf16[256,512]{1,0:T(8,128)(2,1)} %do_ref.1) | copy-start | bytes 786436
  4.4 0.7 %copy-start.4 = (s32[4,4]{1,0:T(4,128)S(1)}, s32[4,4]{1,0:T(4,128)}, u32[]{:S(2)}) copy-start(s32[4,4]{1,0:T(4,128)} %offsets.1) | copy-start | bytes 196
  5.1 0.7 %copy-start.5 = (s32[4]{0:T(128)S(1)}, s32[4]{0:T(128)}, u32[]{:S(2)}) copy-start(s32[4]{0:T(128)} %window.1) | copy-start | bytes 52

commit v2 on v1

--- a/solution.py
+++ b/solution.py
@@ -24,14 +24,14 @@
 
 def kernel(
     size, heads, far,
-    window, offsets, q_ref, k_ref, v_ref, do_ref,
+    window_hbm, offsets_hbm, q_hbm, k_hbm, v_hbm, do_hbm,
     att_ref, gq_ref, gk_ref, gv_ref,
-    own, rx1, rx2, rx4, rxf,
+    window, offsets, q_ref, do_ref, tri_low, own, rx1, rx2, rx4, rxf,
     tg1, tg4, ts2, tgf, rg1, rg4, rs2, rgf, hold2, acc,
-    send, recv,
+    send, recv, load, load_small,
 ):
     f32, bf16 = jnp.float32, jnp.bfloat16
-    rows = q_ref.shape[0]
+    rows = q_hbm.shape[0]
     r = lax.axis_index("ctx")
     odd = lax.rem(r, 2) == 1
     even = jnp.logical_not(odd)
@@ -75,6 +75,27 @@
     def gfar_down(n, h):
         return copy(K_GFAR + n, h, tgf.at[n, h], rgf.at[n, h], r - far[n])
 
+    loads = []
+    for h in range(heads):
+        cols = slice(h * HEAD, (h + 1) * HEAD)
+        loads.append([
+            pltpu.make_async_copy(src.at[:, cols], dst, load.at[h, n])
+            for n, (src, dst) in enumerate((
+                (k_hbm, own.at[h, 0]), (v_hbm, own.at[h, 1]),
+                (q_hbm, q_ref.at[h]), (do_hbm, do_ref.at[h]),
+            ))
+        ])
+    small_copies = [
+        pltpu.make_async_copy(offsets_hbm, offsets, load_small.at[0]),
+        pltpu.make_async_copy(window_hbm, window, load_small.at[1]),
+    ]
+    for pair in (slice(0, 2), slice(2, 4)):
+        for group in loads:
+            for c in group[pair]:
+                c.start()
+    for c in small_copies:
+        c.start()
+
     barrier = pltpu.get_barrier_semaphore()
     pl.semaphore_signal(barrier, inc=1, device_id={"ctx": mate}, device_id_type=MESH)
     count = 1
@@ -86,10 +107,6 @@
             def _(to=to):
                 pl.semaphore_signal(barrier, inc=1, device_id={"ctx": to}, device_id_type=MESH)
 
-    for h in range(heads):
-        cols = slice(h * HEAD, (h + 1) * HEAD)
-        own[h, 0] = k_ref[:, cols]
-        own[h, 1] = v_ref[:, cols]
     for d, buf in ((1, rx1), (2, rx2), (4, rx4)):
 
         @pl.when(r < d)
@@ -115,79 +132,147 @@
             def _(n=n):
                 far_up(n, h).start()
 
+    def loaded(h):
+        for c in loads[h][:2]:
+            c.wait()
+
+    loaded(0)
     start_own(0)
+    loaded(1)
     start_own(1)
+    for h in range(2, heads):
+        loaded(h)
 
     @pl.when(even)
     def _():
         for h in range(heads):
             prev_own(h).start()
 
-    key_i = lax.broadcasted_iota(jnp.int32, (rows, rows), 0)
-    query_i = lax.broadcasted_iota(jnp.int32, (rows, rows), 1)
+    for group in loads:
+        for c in group[2:]:
+            c.wait()
+
+    query_i = lax.broadcasted_iota(jnp.int32, (rows, rows), 0)
+    key_i = lax.broadcasted_iota(jnp.int32, (rows, rows), 1)
     diff = key_i - query_i
     tri = diff <= 0
-    key_block = key_i // BLOCK
-    query_block = lax.broadcasted_iota(jnp.int32, (1, rows), 1) // BLOCK
+    tri_low[0] = jnp.where(tri, 1.0, 0.0).astype(bf16)
+    tri_low[1] = jnp.where(diff >= 0, 1.0, 0.0).astype(bf16)
     dists = (2, 4) + far
-    picks = []
-    for j, d in enumerate(dists):
-        pick = jnp.zeros((1, rows), jnp.int32)
-        for p in range(rows // BLOCK):
-            inside = p + d * (rows // BLOCK) - offsets[p, j]
-            pick = jnp.where(query_block == p, inside, pick)
-        picks.append(jnp.where(r >= d, pick, -1))
+    wide_log = len(dists) * BLOCK
+    lane = lax.broadcasted_iota(jnp.int32, (1, wide_log), 1) // BLOCK
+    log_ok = functools.reduce(
+        jnp.logical_or, [(lane == j) & (r >= d) for j, d in enumerate(dists)]
+    )
+    groups = rows // BLOCK
+    for c in small_copies:
+        c.wait()
+    one_row = lax.broadcasted_iota(jnp.int32, (1, HEAD), 1) * 0
+    chosen = [
+        [
+            [
+                jnp.where(one_row + (p + d * groups - offsets[p, j]) == place, 1.0, 0.0)
+                for place in range(groups)
+            ]
+            for j, d in enumerate(dists)
+        ]
+        for p in range(groups)
+    ]
+    chosen_low = [[[x.astype(bf16) for x in y] for y in z] for z in chosen]
+
+    def block(x, p):
+        return x[p * BLOCK:(p + 1) * BLOCK]
 
     def compute(h):
         cols = slice(h * HEAD, (h + 1) * HEAD)
-        q = q_ref[:, cols]
-        do = do_ref[:, cols]
-        sources = [own[h], rx1[h], rx2[h], rx4[h]] + [rxf[n, h] for n in range(len(far))]
-        ks = [x[0] for x in sources]
-        vs = [x[1] for x in sources]
+        q = q_ref[h]
+        do = do_ref[h]
+        far_bufs = [rx2.at[h], rx4.at[h]] + [rxf.at[n, h] for n in range(len(far))]
+
+        def picked(which):
+            arrays = [buf[which] for buf in far_bufs[:len(dists)]]
+
+            def pick(p, j):
+                terms = [
+                    block(arrays[j], place) * chosen_low[p][j][place] for place in range(groups)
+                ]
+                return functools.reduce(jnp.add, terms)
+
+            return [
+                jnp.concatenate([pick(p, j) for j in range(len(dists))], 0)
+                for p in range(groups)
+            ]
+
+        k_own, k_prev, k_log = own[h, 0], rx1[h, 0], picked(0)
+        v_own, v_prev, v_log = own[h, 1], rx1[h, 1], picked(1)
+
+        def against(x, a, b, log):
+            near = jnp.where(tri, dot(x, a, NT), dot(x, b, NT))
+            return near, jnp.concatenate(
+                [dot(block(x, p), log[p], NT) for p in range(groups)], 0
+            )
+
+        def weighted(xa, xb, xl, a, b, log):
+            return dot(xa, a, NN) + dot(xb, b, NN) + jnp.concatenate(
+                [dot(block(xl, p), log[p], NN) for p in range(groups)], 0
+            )
+
         w = window[h]
         limit = jnp.where(r >= 1, rows - w, 2 * rows)
         ok_win = (tri & (diff > -w)) | (diff > limit)
-        raw = [dot(k, q, NT) for k in ks]
-        scores = [jnp.where(ok_win, jnp.where(tri, raw[0], raw[1]), NEG)]
-        for pick, s in zip(picks, raw[2:]):
-            scores.append(jnp.where(key_block == pick, s, NEG))
-        top = functools.reduce(jnp.maximum, [jnp.max(s, 0, keepdims=True) for s in scores])
+        s_win, s_log = against(q, k_own, k_prev, k_log)
+        s_win = jnp.where(ok_win, s_win, NEG)
+        s_log = jnp.where(log_ok, s_log, NEG)
+        top = jnp.maximum(jnp.max(s_win, 1, keepdims=True), jnp.max(s_log, 1, keepdims=True))
         c = scale * math.log2(math.e)
-        weights = [jnp.exp2((s - top) * c) for s in scores]
-        total = functools.reduce(jnp.add, [jnp.sum(x, 0, keepdims=True) for x in weights])
-        inv = 1.0 / total
-        probs = [x * inv for x in weights]
-
-        def spread(parts):
-            first = parts[0]
-            cut = [jnp.where(tri, first, 0.0), jnp.where(tri, 0.0, first)] + parts[1:]
-            return [x.astype(bf16) for x in cut]
-
-        p_low = spread(probs)
-        v_all = jnp.concatenate(vs, 0)
-        out_t = dot(v_all, jnp.concatenate(p_low, 0), TN)
-        att = out_t.T.astype(bf16)
+        w_win = jnp.exp2((s_win - top) * c)
+        w_log = jnp.exp2((s_log - top) * c)
+        inv = 1.0 / (jnp.sum(w_win, 1, keepdims=True) + jnp.sum(w_log, 1, keepdims=True))
+        p_win = w_win * inv
+        p_log = w_log * inv
+        low = p_win.astype(bf16)
+        low_own = low * tri_low[0]
+        low_log = p_log.astype(bf16)
+        att = weighted(low_own, low - low_own, low_log, v_own, v_prev, v_log).astype(bf16)
         att_ref[:, cols] = att
-        delta = jnp.sum((att.astype(f32) * do.astype(f32)).T, 0, keepdims=True)
-        raw = [dot(v, do, NT) for v in vs]
-        dprobs = [jnp.where(tri, raw[0], raw[1])] + raw[2:]
-        ds = spread([p * (x - delta) for p, x in zip(probs, dprobs)])
-        gq = dot(jnp.concatenate(ks, 0), jnp.concatenate(ds, 0), TN) * scale
-        gq_ref[:, cols] = gq.T.astype(bf16)
-        dk = [dot(x, q, NN) * scale for x in ds]
-        dv = [dot(x, do, NN) for x in p_low]
-        acc[h, 0] = dk[0]
-        acc[h, 1] = dv[0]
-        tg1[h, 0] = dk[1].astype(bf16)
-        tg1[h, 1] = dv[1].astype(bf16)
-        hold2[h, 0] = dk[2]
-        hold2[h, 1] = dv[2]
-        tg4[h, 0] = dk[3].astype(bf16)
-        tg4[h, 1] = dv[3].astype(bf16)
-        for n in range(len(far)):
-            tgf[n, h, 0] = dk[4 + n].astype(bf16)
-            tgf[n, h, 1] = dv[4 + n].astype(bf16)
+
+        def transposed(near, log, x):
+            flip = near.T
+            flip_own = flip * tri_low[1]
+            return dot(flip_own, x, NN), dot(flip - flip_own, x, NN), [
+                dot(block(log, p), block(x, p), TN) for p in range(groups)
+            ]
+
+        def scattered(parts, j):
+            pieces = [block(x, j) for x in parts]
+            return jnp.concatenate(
+                [
+                    functools.reduce(
+                        jnp.add, [pieces[p] * chosen[p][j][place] for p in range(groups)]
+                    )
+                    for place in range(groups)
+                ],
+                0,
+            )
+
+        def keep(which, near, prev, log, factor):
+            acc[h, which] = near * factor
+            tg1[h, which] = (prev * factor).astype(bf16)
+            hold2[h, which] = scattered(log, 0) * factor
+            if len(dists) > 1:
+                tg4[h, which] = (scattered(log, 1) * factor).astype(bf16)
+            for n in range(len(far)):
+                tgf[n, h, which] = (scattered(log, 2 + n) * factor).astype(bf16)
+
+        keep(1, *transposed(low, low_log, do), 1.0)
+        delta = jnp.sum(att.astype(f32) * do.astype(f32), 1, keepdims=True)
+        d_win, d_log = against(do, v_own, v_prev, v_log)
+        ds = (p_win * (d_win - delta)).astype(bf16)
+        ds_own = ds * tri_low[0]
+        ds_log = (p_log * (d_log - delta)).astype(bf16)
+        gq = weighted(ds_own, ds - ds_own, ds_log, k_own, k_prev, k_log) * scale
+        gq_ref[:, cols] = gq.astype(bf16)
+        keep(0, *transposed(ds, ds_log, q), scale)
 
         @pl.when(r >= 4)
         def _():
@@ -326,7 +411,7 @@
     nf = max(len(far), 1)
     kinds = 6 + 2 * len(far)
     vmem = pl.BlockSpec(memory_space=pltpu.VMEM)
-    smem = pl.BlockSpec(memory_space=pltpu.SMEM)
+    hbm = pl.BlockSpec(memory_space=pltpu.HBM)
     pack = (heads, 2, rows, HEAD)
     small = pltpu.VMEM(pack, jnp.bfloat16)
     wide = pltpu.VMEM(pack, jnp.float32)
@@ -335,11 +420,19 @@
     return pl.pallas_call(
         functools.partial(kernel, size, heads, far),
         out_shape=(out,) * 4,
-        in_specs=[smem, smem] + [vmem] * 4,
+        in_specs=[hbm] * 6,
         out_specs=(vmem,) * 4,
-        scratch_shapes=[small] * 4 + [more] + [small] * 3 + [more] + [small] * 3 + [more]
+        scratch_shapes=[
+            pltpu.SMEM(window.shape, jnp.int32),
+            pltpu.SMEM(offsets.shape, jnp.int32),
+            pltpu.VMEM((heads, rows, HEAD), jnp.bfloat16),
+            pltpu.VMEM((heads, rows, HEAD), jnp.bfloat16),
+            pltpu.VMEM((2, rows, rows), jnp.bfloat16),
+        ]
+        + [small] * 4 + [more] + [small] * 3 + [more] + [small] * 3 + [more]
         + [wide] * 2
-        + [pltpu.SemaphoreType.DMA((kinds, heads)), pltpu.SemaphoreType.DMA((kinds, heads))],
+        + [pltpu.SemaphoreType.DMA((kinds, heads)), pltpu.SemaphoreType.DMA((kinds, heads))]
+        + [pltpu.SemaphoreType.DMA((heads, 4)), pltpu.SemaphoreType.DMA((2,))],
         compiler_params=pltpu.CompilerParams(
             collective_id=0, has_side_effects=True, vmem_limit_bytes=48 * 2**20
         ),

time: 52.2 us -> 51.8 us (level)
  no operation moved by 1% of the time
where the time goes in v2:
time: 51.8 us; the launch traced here: 51.6 us
  Pallas kernels  43 us (83%)
  local copies, waits for them, and re-layouts  7.94 us (15%)
  between operations  0.66 us (1%)
    pallas_call x1, Pallas kernels, on_device(): pl.pallas_call(functools.partial(kernel, size, heads, far), out_shape=(ou...  43 us
    unnamed x16, local copies, waits for them, and re-layouts  7.94 us

profile of v2, /device:TPU:0, one launch (start us, length us, event | category | flops | bytes accessed | tf_op | source)
XLA Modules:
  0.0 51.6 jit_solution(11693581357433910774)
XLA Ops:
  0.6 0.0 copy-start
  0.6 0.9 %copy-done = bf16[256,512]{1,0:T(8,128)(2,1)S(1)} copy-done((bf16[256,512]{1,0:T(8,128)(2,1)S(1)}, bf16[256,512]{1,0:T(8,128)(2,1)}, u32[]{:S(2)}) %copy-start) | copy-done | bytes 262168
  1.6 0.0 copy-start.1
  1.6 0.9 %copy-done.1 = bf16[256,512]{1,0:T(8,128)(2,1)S(1)} copy-done((bf16[256,512]{1,0:T(8,128)(2,1)S(1)}, bf16[256,512]{1,0:T(8,128)(2,1)}, u32[]{:S(2)}) %copy-start.1) | copy-done | bytes 262168
  2.5 0.0 copy-start.2
  2.5 0.9 %copy-done.2 = bf16[256,512]{1,0:T(8,128)(2,1)S(1)} copy-done((bf16[256,512]{1,0:T(8,128)(2,1)S(1)}, bf16[256,512]{1,0:T(8,128)(2,1)}, u32[]{:S(2)}) %copy-start.2) | copy-done | bytes 262168
  3.5 0.0 copy-start.3
  3.5 0.9 %copy-done.3 = bf16[256,512]{1,0:T(8,128)(2,1)S(1)} copy-done((bf16[256,512]{1,0:T(8,128)(2,1)S(1)}, bf16[256,512]{1,0:T(8,128)(2,1)}, u32[]{:S(2)}) %copy-start.3) | copy-done | bytes 262168
  4.4 0.0 copy-start.4
  4.4 0.7 %copy-done.4 = s32[4,4]{1,0:T(4,128)S(1)} copy-done((s32[4,4]{1,0:T(4,128)S(1)}, s32[4,4]{1,0:T(4,128)}, u32[]{:S(2)}) %copy-start.4) | copy-done | bytes 88
  5.1 0.0 copy-start.5
  5.1 0.7 %copy-done.5 = s32[4]{0:T(128)S(1)} copy-done((s32[4]{0:T(128)S(1)}, s32[4]{0:T(128)}, u32[]{:S(2)}) %copy-start.5) | copy-done | bytes 40
  5.8 43.0 %shard_map.93 = (bf16[256,512]{1,0:T(8,128)(2,1)S(1)}, bf16[256,512]{1,0:T(8,128)(2,1)S(1)}, bf16[256,512]{1,0:T(8,128)(2,1)S(1)}, bf16[256,512]{1,0:T(8,128)(2,1)S(1)}) custom-call(s32[4]{0:T(128)S(1)} %copy-done.5, s32[4,4]{1,0:T(4,128)S(1)} %copy-done.4, bf16[256,512]{1,0:T(8,128)(2,1)S(1)} %copy-done, bf16[256,512]{1,0:T(8,128)(2,1)S(1)} %copy-done.1, ...), custom_call_target="tpu_custom_call" | custom-call | flops 1610612736 | bytes 2097152 | tf_op jit(solution)/shard_map/pallas_call | solution.py:420
  48.8 0.7 %copy.14 = bf16[256,512]{1,0:T(8,128)(2,1)} copy(bf16[256,512]{1,0:T(8,128)(2,1)S(1)} %get-tuple-element.8) | data formatting | bytes 524288
  49.5 0.7 %copy.15 = bf16[256,512]{1,0:T(8,128)(2,1)} copy(bf16[256,512]{1,0:T(8,128)(2,1)S(1)} %get-tuple-element.9) | data formatting | bytes 524288
  50.2 0.7 %copy.16 = bf16[256,512]{1,0:T(8,128)(2,1)} copy(bf16[256,512]{1,0:T(8,128)(2,1)S(1)} %get-tuple-element.10) | data formatting | bytes 524288
  50.9 0.7 %copy.17 = bf16[256,512]{1,0:T(8,128)(2,1)} copy(bf16[256,512]{1,0:T(8,128)(2,1)S(1)} %get-tuple-element.11) | data formatting | bytes 524288
Async XLA Ops:
  0.6 1.0 %copy-start = (bf16[256,512]{1,0:T(8,128)(2,1)S(1)}, bf16[256,512]{1,0:T(8,128)(2,1)}, u32[]{:S(2)}) copy-start(bf16[256,512]{1,0:T(8,128)(2,1)} %q_hbm.1) | copy-start | bytes 786436
  1.6 0.9 %copy-start.1 = (bf16[256,512]{1,0:T(8,128)(2,1)S(1)}, bf16[256,512]{1,0:T(8,128)(2,1)}, u32[]{:S(2)}) copy-start(bf16[256,512]{1,0:T(8,128)(2,1)} %k_hbm.1) | copy-start | bytes 786436
  2.5 0.9 %copy-start.2 = (bf16[256,512]{1,0:T(8,128)(2,1)S(1)}, bf16[256,512]{1,0:T(8,128)(2,1)}, u32[]{:S(2)}) copy-start(bf16[256,512]{1,0:T(8,128)(2,1)} %v_hbm.1) | copy-start | bytes 786436
  3.5 0.9 %copy-start.3 = (bf16[256,512]{1,0:T(8,128)(2,1)S(1)}, bf16[256,512]{1,0:T(8,128)(2,1)}, u32[]{:S(2)}) copy-start(bf16[256,512]{1,0:T(8,128)(2,1)} %do_hbm.1) | copy-start | bytes 786436
  4.4 0.7 %copy-start.4 = (s32[4,4]{1,0:T(4,128)S(1)}, s32[4,4]{1,0:T(4,128)}, u32[]{:S(2)}) copy-start(s32[4,4]{1,0:T(4,128)} %offsets_hbm.1) | copy-start | bytes 196
  5.1 0.7 %copy-start.5 = (s32[4]{0:T(128)S(1)}, s32[4]{0:T(128)}, u32[]{:S(2)}) copy-start(s32[4]{0:T(128)} %window_hbm.1) | copy-start | bytes 52

commit v3 on v2

--- a/solution.py
+++ b/solution.py
@@ -12,6 +12,7 @@
 LEVELS = 4
 HEAD = 128
 NEG = -1e30
+AHEAD = 3
 MESH = pl.DeviceIdType.MESH
 NT = (((1,), (1,)), ((), ()))
 TN = (((0,), (0,)), ((), ()))
@@ -25,10 +26,10 @@
 def kernel(
     size, heads, far,
     window_hbm, offsets_hbm, q_hbm, k_hbm, v_hbm, do_hbm,
-    att_ref, gq_ref, gk_ref, gv_ref,
-    window, offsets, q_ref, do_ref, tri_low, own, rx1, rx2, rx4, rxf,
+    att_hbm, gq_hbm, gk_hbm, gv_hbm,
+    staged, window, offsets, q_ref, do_ref, tri_low, own, rx1, rx2, rx4, rxf,
     tg1, tg4, ts2, tgf, rg1, rg4, rs2, rgf, hold2, acc,
-    send, recv, load, load_small,
+    send, recv, load, load_small, store,
 ):
     f32, bf16 = jnp.float32, jnp.bfloat16
     rows = q_hbm.shape[0]
@@ -48,32 +49,41 @@
             device_id={"ctx": to}, device_id_type=MESH,
         )
 
-    def own_up(h):
-        return copy(K_OWN, h, own.at[h], rx2.at[h], r + 2)
-
-    def relay_up(h):
-        return copy(K_REL, h, rx2.at[h], rx4.at[h], r + 2)
-
-    def prev_own(h):
-        return copy(K_PRV, h, own.at[h], rx1.at[h], mate)
-
-    def prev_relay(h):
-        return copy(K_PRV, h, rx2.at[h], rx1.at[h], mate)
-
-    def far_up(n, h):
-        return copy(K_FAR + n, h, own.at[h], rxf.at[n, h], r + far[n])
-
-    def g4_down(h):
-        return copy(K_G4, h, tg4.at[h], rg4.at[h], r - 2)
-
-    def s2_down(h):
-        return copy(K_S2, h, ts2.at[h], rs2.at[h], r - 2)
-
-    def g1_mate(h):
-        return copy(K_G1, h, tg1.at[h], rg1.at[h], mate)
-
-    def gfar_down(n, h):
-        return copy(K_GFAR + n, h, tgf.at[n, h], rgf.at[n, h], r - far[n])
+    def piece(buf, i):
+        return buf.at[i // 2, i % 2]
+
+    def own_up(i):
+        return copy(K_OWN, i, piece(own, i), piece(rx2, i), r + 2)
+
+    def relay_up(i):
+        return copy(K_REL, i, piece(rx2, i), piece(rx4, i), r + 2)
+
+    def prev_own(i):
+        return copy(K_PRV, i, piece(own, i), piece(rx1, i), mate)
+
+    def prev_relay(i):
+        return copy(K_PRV, i, piece(rx2, i), piece(rx1, i), mate)
+
+    def far_up(n, i):
+        return copy(K_FAR + n, i, piece(own, i), piece(rxf.at[n], i), r + far[n])
+
+    def g4_down(i):
+        return copy(K_G4, i, piece(tg4, i), piece(rg4, i), r - 2)
+
+    def s2_down(i):
+        return copy(K_S2, i, piece(ts2, i), piece(rs2, i), r - 2)
+
+    def g1_mate(i):
+        return copy(K_G1, i, piece(tg1, i), piece(rg1, i), mate)
+
+    def gfar_down(n, i):
+        return copy(K_GFAR + n, i, piece(tgf.at[n], i), piece(rgf.at[n], i), r - far[n])
+
+    def result(n, h):
+        out = (att_hbm, gq_hbm, gk_hbm, gv_hbm)[n]
+        return pltpu.make_async_copy(
+            staged.at[n, h], out.at[:, h * HEAD:(h + 1) * HEAD], store.at[n, h]
+        )
 
     loads = []
     for h in range(heads):
@@ -121,33 +131,27 @@
 
     pl.semaphore_wait(barrier, count)
 
-    def start_own(h):
+    pieces = 2 * heads
+
+    def start_own(i):
+        loads[i // 2][i % 2].wait()
+
         @pl.when(has_up)
         def _():
-            own_up(h).start()
+            own_up(i).start()
+
+        @pl.when(even)
+        def _():
+            prev_own(i).start()
 
         for n in range(len(far)):
 
             @pl.when(r + far[n] < size)
             def _(n=n):
-                far_up(n, h).start()
-
-    def loaded(h):
-        for c in loads[h][:2]:
-            c.wait()
-
-    loaded(0)
-    start_own(0)
-    loaded(1)
-    start_own(1)
-    for h in range(2, heads):
-        loaded(h)
-
-    @pl.when(even)
-    def _():
-        for h in range(heads):
-            prev_own(h).start()
-
+                far_up(n, i).start()
+
+    for i in range(AHEAD):
+        start_own(i)
     for group in loads:
         for c in group[2:]:
             c.wait()
@@ -183,8 +187,22 @@
     def block(x, p):
         return x[p * BLOCK:(p + 1) * BLOCK]
 
+    def send_back(i):
+        @pl.when(r >= 4)
+        def _():
+            g4_down(i).start()
+
+        @pl.when(r >= 1)
+        def _():
+            g1_mate(i).start()
+
+        for n in range(len(far)):
+
+            @pl.when(r >= far[n])
+            def _(n=n):
+                gfar_down(n, i).start()
+
     def compute(h):
-        cols = slice(h * HEAD, (h + 1) * HEAD)
         q = q_ref[h]
         do = do_ref[h]
         far_bufs = [rx2.at[h], rx4.at[h]] + [rxf.at[n, h] for n in range(len(far))]
@@ -203,8 +221,8 @@
                 for p in range(groups)
             ]
 
+        arrive(2 * h)
         k_own, k_prev, k_log = own[h, 0], rx1[h, 0], picked(0)
-        v_own, v_prev, v_log = own[h, 1], rx1[h, 1], picked(1)
 
         def against(x, a, b, log):
             near = jnp.where(tri, dot(x, a, NT), dot(x, b, NT))
@@ -233,9 +251,6 @@
         low = p_win.astype(bf16)
         low_own = low * tri_low[0]
         low_log = p_log.astype(bf16)
-        att = weighted(low_own, low - low_own, low_log, v_own, v_prev, v_log).astype(bf16)
-        att_ref[:, cols] = att
-
         def transposed(near, log, x):
             flip = near.T
             flip_own = flip * tri_low[1]
@@ -265,142 +280,161 @@
                 tgf[n, h, which] = (scattered(log, 2 + n) * factor).astype(bf16)
 
         keep(1, *transposed(low, low_log, do), 1.0)
+        send_back(2 * h + 1)
+        yield
+        arrive(2 * h + 1)
+        v_own, v_prev, v_log = own[h, 1], rx1[h, 1], picked(1)
+        att = weighted(low_own, low - low_own, low_log, v_own, v_prev, v_log).astype(bf16)
+        staged[0, h] = att
+        result(0, h).start()
         delta = jnp.sum(att.astype(f32) * do.astype(f32), 1, keepdims=True)
         d_win, d_log = against(do, v_own, v_prev, v_log)
         ds = (p_win * (d_win - delta)).astype(bf16)
         ds_own = ds * tri_low[0]
         ds_log = (p_log * (d_log - delta)).astype(bf16)
+        keep(0, *transposed(ds, ds_log, q), scale)
+        send_back(2 * h)
         gq = weighted(ds_own, ds - ds_own, ds_log, k_own, k_prev, k_log) * scale
-        gq_ref[:, cols] = gq.astype(bf16)
-        keep(0, *transposed(ds, ds_log, q), scale)
+        staged[1, h] = gq.astype(bf16)
+        result(1, h).start()
+        yield
+
+    def combine(i):
+        h, w = i // 2, i % 2
+
+        @pl.when((r >= 2) & has_up)
+        def _():
+            g4_down(i).wait_recv()
+            hold2[h, w] = hold2[h, w] + rg4[h, w].astype(f32)
+
+        @pl.when(odd & (r >= 3))
+        def _():
+            g1_mate(i).wait_recv()
+            hold2[h, w] = hold2[h, w] + rg1[h, w].astype(f32)
+
+        @pl.when(r >= 2)
+        def _():
+            ts2[h, w] = hold2[h, w].astype(bf16)
+            s2_down(i).start()
+
+    def relay(i):
+        @pl.when(r >= 2)
+        def _():
+            own_up(i).wait_recv()
+
+        @pl.when((r >= 2) & has_up)
+        def _():
+            relay_up(i).start()
+
+        @pl.when(odd & (r >= 3))
+        def _():
+            prev_relay(i).start()
+
+        if i + AHEAD < pieces:
+            start_own(i + AHEAD)
+
+    def arrive(i):
+        @pl.when(r >= 1)
+        def _():
+            prev_own(i).wait_recv()
 
         @pl.when(r >= 4)
         def _():
-            g4_down(h).start()
-
-        @pl.when(r >= 1)
-        def _():
-            g1_mate(h).start()
+            relay_up(i).wait_recv()
 
         for n in range(len(far)):
 
             @pl.when(r >= far[n])
             def _(n=n):
-                gfar_down(n, h).start()
-
-    def combine(h):
+                far_up(n, i).wait_recv()
+
+    def finish(i):
+        h, w = i // 2, i % 2
+
+        @pl.when(even)
+        def _():
+            g1_mate(i).wait_recv()
+            acc[h, w] = acc[h, w] + rg1[h, w].astype(f32)
+
+        for n in range(len(far)):
+
+            @pl.when(r + far[n] < size)
+            def _(n=n):
+                gfar_down(n, i).wait_recv()
+                acc[h, w] = acc[h, w] + rgf[n, h, w].astype(f32)
+
+        @pl.when(has_up)
+        def _():
+            s2_down(i).wait_recv()
+            acc[h, w] = acc[h, w] + rs2[h, w].astype(f32)
+
+        staged[2 + w, h] = acc[h, w].astype(bf16)
+        result(2 + w, h).start()
+
+    back = [i for h in range(heads) for i in (2 * h + 1, 2 * h)]
+    steps = [compute(h) for h in range(heads)]
+    for i in range(AHEAD):
+        relay(i)
+    for i in range(pieces):
+        next(steps[i // 2])
+        if i + AHEAD < pieces:
+            relay(i + AHEAD)
+        if i >= 1:
+            combine(back[i - 1])
+    combine(back[-1])
+    for i in back:
+        finish(i)
+
+    for i in range(pieces):
+
+        @pl.when(has_up)
+        def _(i=i):
+            own_up(i).wait_send()
+
         @pl.when((r >= 2) & has_up)
-        def _():
-            g4_down(h).wait_recv()
-            hold2[h] = hold2[h] + rg4[h].astype(f32)
-
-        @pl.when(odd & (r >= 3))
-        def _():
-            g1_mate(h).wait_recv()
-            hold2[h] = hold2[h] + rg1[h].astype(f32)
+        def _(i=i):
+            relay_up(i).wait_send()
+
+        @pl.when(even | (r >= 3))
+        def _(i=i):
+            prev_own(i).wait_send()
+
+        @pl.when(r >= 4)
+        def _(i=i):
+            g4_down(i).wait_send()
 
         @pl.when(r >= 2)
-        def _():
-            ts2[h] = hold2[h].astype(bf16)
-            s2_down(h).start()
-
-    for i in range(heads + 1):
-        if i < heads:
-
-            @pl.when(r >= 2)
-            def _(i=i):
-                own_up(i).wait_recv()
-
-            @pl.when((r >= 2) & has_up)
-            def _(i=i):
-                relay_up(i).start()
-
-            @pl.when(odd & (r >= 3))
-            def _(i=i):
-                prev_relay(i).start()
-
-            if i + 2 < heads:
-                start_own(i + 2)
-        if i >= 1:
-            h = i - 1
-
-            @pl.when(r >= 1)
-            def _(h=h):
-                prev_own(h).wait_recv()
-
-            @pl.when(r >= 4)
-            def _(h=h):
-                relay_up(h).wait_recv()
-
-            for n in range(len(far)):
-
-                @pl.when(r >= far[n])
-                def _(n=n, h=h):
-                    far_up(n, h).wait_recv()
-
-            compute(h)
-        if i >= 2:
-            combine(i - 2)
-    combine(heads - 1)
-
-    for h in range(heads):
-        cols = slice(h * HEAD, (h + 1) * HEAD)
-
-        @pl.when(even)
-        def _(h=h):
-            g1_mate(h).wait_recv()
-            acc[h] = acc[h] + rg1[h].astype(f32)
+        def _(i=i):
+            s2_down(i).wait_send()
+
+        @pl.when(r >= 1)
+        def _(i=i):
+            g1_mate(i).wait_send()
 
         for n in range(len(far)):
 
             @pl.when(r + far[n] < size)
-            def _(n=n, h=h):
-                gfar_down(n, h).wait_recv()
-                acc[h] = acc[h] + rgf[n, h].astype(f32)
-
-        @pl.when(has_up)
-        def _(h=h):
-            s2_down(h).wait_recv()
-            acc[h] = acc[h] + rs2[h].astype(f32)
-
-        gk_ref[:, cols] = acc[h, 0].astype(bf16)
-        gv_ref[:, cols] = acc[h, 1].astype(bf16)
-
-    for h in range(heads):
-
-        @pl.when(has_up)
-        def _(h=h):
-            own_up(h).wait_send()
-
-        @pl.when((r >= 2) & has_up)
-        def _(h=h):
-            relay_up(h).wait_send()
-
-        @pl.when(even | (r >= 3))
-        def _(h=h):
-            prev_own(h).wait_send()
-
-        @pl.when(r >= 4)
-        def _(h=h):
-            g4_down(h).wait_send()
-
-        @pl.when(r >= 2)
-        def _(h=h):
-            s2_down(h).wait_send()
-
-        @pl.when(r >= 1)
-        def _(h=h):
-            g1_mate(h).wait_send()
-
-        for n in range(len(far)):
-
-            @pl.when(r + far[n] < size)
-            def _(n=n, h=h):
-                far_up(n, h).wait_send()
+            def _(n=n, i=i):
+                far_up(n, i).wait_send()
 
             @pl.when(r >= far[n])
-            def _(n=n, h=h):
-                gfar_down(n, h).wait_send()
+            def _(n=n, i=i):
+                gfar_down(n, i).wait_send()
+
+    for n in range(4):
+        for h in range(heads):
+            result(n, h).wait()
+
+
+def copy_out(*refs):
+    sems = refs[-1]
+    copies = [
+        pltpu.make_async_copy(refs[n], refs[4 + n], sems.at[n]) for n in range(4)
+    ]
+    for c in copies:
+        c.start()
+    for c in copies:
+        c.wait()
 
 
 def on_device(queries, keys, values, grad_out, window, offsets):
@@ -410,19 +444,19 @@
     far = tuple(2 ** (j + 1) for j in range(2, LEVELS) if 2 ** (j + 1) < size)
     nf = max(len(far), 1)
     kinds = 6 + 2 * len(far)
-    vmem = pl.BlockSpec(memory_space=pltpu.VMEM)
     hbm = pl.BlockSpec(memory_space=pltpu.HBM)
     pack = (heads, 2, rows, HEAD)
     small = pltpu.VMEM(pack, jnp.bfloat16)
     wide = pltpu.VMEM(pack, jnp.float32)
     more = pltpu.VMEM((nf,) + (pack if far else (1, 2, 16, HEAD)), jnp.bfloat16)
     out = jax.ShapeDtypeStruct((rows, feat), jnp.bfloat16)
-    return pl.pallas_call(
+    parts = pl.pallas_call(
         functools.partial(kernel, size, heads, far),
         out_shape=(out,) * 4,
         in_specs=[hbm] * 6,
-        out_specs=(vmem,) * 4,
+        out_specs=(hbm,) * 4,
         scratch_shapes=[
+            pltpu.VMEM((4, heads, rows, HEAD), jnp.bfloat16),
             pltpu.SMEM(window.shape, jnp.int32),
             pltpu.SMEM(offsets.shape, jnp.int32),
             pltpu.VMEM((heads, rows, HEAD), jnp.bfloat16),
@@ -431,10 +465,11 @@
         ]
         + [small] * 4 + [more] + [small] * 3 + [more] + [small] * 3 + [more]
         + [wide] * 2
-        + [pltpu.SemaphoreType.DMA((kinds, heads)), pltpu.SemaphoreType.DMA((kinds, heads))]
-        + [pltpu.SemaphoreType.DMA((heads, 4)), pltpu.SemaphoreType.DMA((2,))],
+        + [pltpu.SemaphoreType.DMA((kinds, 2 * heads)), pltpu.SemaphoreType.DMA((kinds, 2 * heads))]
+        + [pltpu.SemaphoreType.DMA((heads, 4)), pltpu.SemaphoreType.DMA((2,))]
+        + [pltpu.SemaphoreType.DMA((4, heads))],
         compiler_params=pltpu.CompilerParams(
-            collective_id=0, has_side_effects=True, vmem_limit_bytes=48 * 2**20
+            collective_id=0, has_side_effects=True, vmem_limit_bytes=63 * 2**20
         ),
         cost_estimate=pl.CostEstimate(
             flops=12 * heads * rows * rows * HEAD * (4 + len(far)),
@@ -442,6 +477,17 @@
             transcendentals=heads * rows * rows * (3 + len(far)),
         ),
     )(window, offsets, queries, keys, values, grad_out)
+    return pl.pallas_call(
+        copy_out,
+        out_shape=(out,) * 4,
+        in_specs=[hbm] * 4,
+        out_specs=(hbm,) * 4,
+        scratch_shapes=[pltpu.SemaphoreType.DMA((4,))],
+        compiler_params=pltpu.CompilerParams(vmem_limit_bytes=63 * 2**20),
+        cost_estimate=pl.CostEstimate(
+            flops=0, bytes_accessed=16 * rows * feat, transcendentals=0
+        ),
+    )(*parts)
 
 
 def solution(mesh):

time: 51.8 us -> 74.2 us (1.43)
  Pallas kernels: 43 us -> 73.5 us
  local copies, waits for them, and re-layouts: 7.94 us -> 0 us
    pallas_call x0 -> x1, Pallas kernels: none -> 32.9 us  [on_device(): pl.pallas_call(copy_out, out_shape=(out,) * 4, in_specs=[hbm] * 4, out_sp...]
    unnamed x16 -> x0, local copies, waits for them, and re-layouts: 7.94 us -> none
    pallas_call x1, Pallas kernels: 43 us -> 40.6 us  [on_device(): pl.pallas_call(functools.partial(kernel, size, heads, far), out_shape=(ou...]
where the time goes in v3:
time: 74.2 us; the launch traced here: 74.1 us
  Pallas kernels  73.5 us (99%)
    pallas_call x1, Pallas kernels, on_device(): pl.pallas_call(functools.partial(kernel, size, heads, far), out_shape=(ou...  40.6 us
    pallas_call x1, Pallas kernels, on_device(): pl.pallas_call(copy_out, out_shape=(out,) * 4, in_specs=[hbm] * 4, out_sp...  32.9 us

profile of v3, /device:TPU:0, one launch (start us, length us, event | category | flops | bytes accessed | tf_op | source)
XLA Modules:
  0.0 74.1 jit_solution(2812339885159686533)
XLA Ops:
  0.6 40.6 %shard_map.93 = (bf16[256,512]{1,0:T(8,128)(2,1)}, bf16[256,512]{1,0:T(8,128)(2,1)}, bf16[256,512]{1,0:T(8,128)(2,1)}, bf16[256,512]{1,0:T(8,128)(2,1)}) custom-call(s32[4]{0:T(128)} %window_hbm.1, s32[4,4]{1,0:T(4,128)} %offsets_hbm.1, bf16[256,512]{1,0:T(8,128)(2,1)} %q_hbm.1, bf16[256,512]{1,0:T(8,128)(2,1)} %k_hbm.1, bf16[256,512]{1,0:T(8,128)(2,1)} %v_hbm.1, ...), custom_call_target="tpu_custom_call" | custom-call | flops 1610612736 | bytes 2097152 | tf_op jit(solution)/shard_map/pallas_call | solution.py:453
  41.2 32.9 %shard_map.94 = (bf16[256,512]{1,0:T(8,128)(2,1)}, bf16[256,512]{1,0:T(8,128)(2,1)}, bf16[256,512]{1,0:T(8,128)(2,1)}, bf16[256,512]{1,0:T(8,128)(2,1)}) custom-call(bf16[256,512]{1,0:T(8,128)(2,1)} %get-tuple-element.8.refs_0_, bf16[256,512]{1,0:T(8,128)(2,1)} %get-tuple-element.9.refs_1_, bf16[256,512]{1,0:T(8,128)(2,1)} %get-tuple-element.10.refs_2_, ...), custom_call_target="tpu_custom_call" | custom-call | bytes 2097152 | tf_op jit(solution)/shard_map/pallas_call | solution.py:480

commit v4 on v3

--- a/solution.py
+++ b/solution.py
@@ -12,7 +12,7 @@
 LEVELS = 4
 HEAD = 128
 NEG = -1e30
-AHEAD = 3
+AHEAD = 4
 MESH = pl.DeviceIdType.MESH
 NT = (((1,), (1,)), ((), ()))
 TN = (((0,), (0,)), ((), ()))
@@ -187,20 +187,21 @@
     def block(x, p):
         return x[p * BLOCK:(p + 1) * BLOCK]
 
-    def send_back(i):
+    def send_far(i):
         @pl.when(r >= 4)
         def _():
             g4_down(i).start()
-
-        @pl.when(r >= 1)
-        def _():
-            g1_mate(i).start()
 
         for n in range(len(far)):
 
             @pl.when(r >= far[n])
             def _(n=n):
                 gfar_down(n, i).start()
+
+    def send_near(i):
+        @pl.when(r >= 1)
+        def _():
+            g1_mate(i).start()
 
     def compute(h):
         q = q_ref[h]
@@ -251,13 +252,6 @@
         low = p_win.astype(bf16)
         low_own = low * tri_low[0]
         low_log = p_log.astype(bf16)
-        def transposed(near, log, x):
-            flip = near.T
-            flip_own = flip * tri_low[1]
-            return dot(flip_own, x, NN), dot(flip - flip_own, x, NN), [
-                dot(block(log, p), block(x, p), TN) for p in range(groups)
-            ]
-
         def scattered(parts, j):
             pieces = [block(x, j) for x in parts]
             return jnp.concatenate(
@@ -270,17 +264,22 @@
                 0,
             )
 
-        def keep(which, near, prev, log, factor):
-            acc[h, which] = near * factor
-            tg1[h, which] = (prev * factor).astype(bf16)
-            hold2[h, which] = scattered(log, 0) * factor
+        def keep(which, near, log, x, factor):
+            i = 2 * h + which
+            parts = [dot(block(log, p), block(x, p), TN) for p in range(groups)]
+            for n in range(len(far)):
+                tgf[n, h, which] = (scattered(parts, 2 + n) * factor).astype(bf16)
             if len(dists) > 1:
-                tg4[h, which] = (scattered(log, 1) * factor).astype(bf16)
-            for n in range(len(far)):
-                tgf[n, h, which] = (scattered(log, 2 + n) * factor).astype(bf16)
-
-        keep(1, *transposed(low, low_log, do), 1.0)
-        send_back(2 * h + 1)
+                tg4[h, which] = (scattered(parts, 1) * factor).astype(bf16)
+            send_far(i)
+            flip = near.T
+            flip_own = flip * tri_low[1]
+            tg1[h, which] = (dot(flip - flip_own, x, NN) * factor).astype(bf16)
+            send_near(i)
+            hold2[h, which] = scattered(parts, 0) * factor
+            acc[h, which] = dot(flip_own, x, NN) * factor
+
+        keep(1, low, low_log, do, 1.0)
         yield
         arrive(2 * h + 1)
         v_own, v_prev, v_log = own[h, 1], rx1[h, 1], picked(1)
@@ -292,8 +291,7 @@
         ds = (p_win * (d_win - delta)).astype(bf16)
         ds_own = ds * tri_low[0]
         ds_log = (p_log * (d_log - delta)).astype(bf16)
-        keep(0, *transposed(ds, ds_log, q), scale)
-        send_back(2 * h)
+        keep(0, ds, ds_log, q, scale)
         gq = weighted(ds_own, ds - ds_own, ds_log, k_own, k_prev, k_log) * scale
         staged[1, h] = gq.astype(bf16)
         result(1, h).start()
@@ -427,13 +425,15 @@
 
 
 def copy_out(*refs):
-    sems = refs[-1]
-    copies = [
-        pltpu.make_async_copy(refs[n], refs[4 + n], sems.at[n]) for n in range(4)
-    ]
-    for c in copies:
+    ins, outs, (held, into, back) = refs[:4], refs[4:8], refs[8:]
+    first = [pltpu.make_async_copy(ins[n], held.at[n], into.at[n]) for n in range(4)]
+    second = [pltpu.make_async_copy(held.at[n], outs[n], back.at[n]) for n in range(4)]
+    for c in first:
         c.start()
-    for c in copies:
+    for n in range(4):
+        first[n].wait()
+        second[n].start()
+    for c in second:
         c.wait()
 
 
@@ -482,7 +482,11 @@
         out_shape=(out,) * 4,
         in_specs=[hbm] * 4,
         out_specs=(hbm,) * 4,
-        scratch_shapes=[pltpu.SemaphoreType.DMA((4,))],
+        scratch_shapes=[
+            pltpu.VMEM((4, rows, feat), jnp.bfloat16),
+            pltpu.SemaphoreType.DMA((4,)),
+            pltpu.SemaphoreType.DMA((4,)),
+        ],
         compiler_params=pltpu.CompilerParams(vmem_limit_bytes=63 * 2**20),
         cost_estimate=pl.CostEstimate(
             flops=0, bytes_accessed=16 * rows * feat, transcendentals=0

time: 74.2 us -> 44.7 us (0.60)
  Pallas kernels: 73.5 us -> 43.9 us
    pallas_call x1, Pallas kernels: 32.9 us -> 1.98 us  [on_device(): pl.pallas_call(copy_out, out_shape=(out,) * 4, in_specs=[hbm] * 4, out_sp...]
    pallas_call x1, Pallas kernels: 40.6 us -> 41.9 us  [on_device(): pl.pallas_call(functools.partial(kernel, size, heads, far), out_shape=(ou...]
where the time goes in v4:
time: 44.7 us; the launch traced here: 44.5 us
  Pallas kernels  43.9 us (98%)
  between operations  0.64 us (1%)
    pallas_call x1, Pallas kernels, on_device(): pl.pallas_call(functools.partial(kernel, size, heads, far), out_shape=(ou...  41.9 us
    pallas_call x1, Pallas kernels, on_device(): pl.pallas_call(copy_out, out_shape=(out,) * 4, in_specs=[hbm] * 4, out_sp...  1.98 us

profile of v4, /device:TPU:0, one launch (start us, length us, event | category | flops | bytes accessed | tf_op | source)
XLA Modules:
  0.0 44.5 jit_solution(15873005712368212256)
XLA Ops:
  0.6 41.9 %shard_map.93 = (bf16[256,512]{1,0:T(8,128)(2,1)}, bf16[256,512]{1,0:T(8,128)(2,1)}, bf16[256,512]{1,0:T(8,128)(2,1)}, bf16[256,512]{1,0:T(8,128)(2,1)}) custom-call(s32[4]{0:T(128)} %window_hbm.1, s32[4,4]{1,0:T(4,128)} %offsets_hbm.1, bf16[256,512]{1,0:T(8,128)(2,1)} %q_hbm.1, bf16[256,512]{1,0:T(8,128)(2,1)} %k_hbm.1, bf16[256,512]{1,0:T(8,128)(2,1)} %v_hbm.1, ...), custom_call_target="tpu_custom_call" | custom-call | flops 1610612736 | bytes 2097152 | tf_op jit(solution)/shard_map/pallas_call | solution.py:453
  42.5 2.0 %shard_map.94 = (bf16[256,512]{1,0:T(8,128)(2,1)}, bf16[256,512]{1,0:T(8,128)(2,1)}, bf16[256,512]{1,0:T(8,128)(2,1)}, bf16[256,512]{1,0:T(8,128)(2,1)}) custom-call(bf16[256,512]{1,0:T(8,128)(2,1)} %get-tuple-element.8.refs_0_, bf16[256,512]{1,0:T(8,128)(2,1)} %get-tuple-element.9.refs_1_, bf16[256,512]{1,0:T(8,128)(2,1)} %get-tuple-element.10.refs_2_, ...), custom_call_target="tpu_custom_call" | custom-call | bytes 2097152 | tf_op jit(solution)/shard_map/pallas_call | solution.py:480

commit v5 on v4

--- a/solution.py
+++ b/solution.py
@@ -12,7 +12,8 @@
 LEVELS = 4
 HEAD = 128
 NEG = -1e30
-AHEAD = 4
+AHEAD = 2
+LAG = 2
 MESH = pl.DeviceIdType.MESH
 NT = (((1,), (1,)), ((), ()))
 TN = (((0,), (0,)), ((), ()))
@@ -377,9 +378,10 @@
         next(steps[i // 2])
         if i + AHEAD < pieces:
             relay(i + AHEAD)
-        if i >= 1:
-            combine(back[i - 1])
-    combine(back[-1])
+        if i >= LAG:
+            combine(back[i - LAG])
+    for i in back[-LAG:]:
+        combine(i)
     for i in back:
         finish(i)
 

time: 44.7 us -> 42.7 us (0.955)
  Pallas kernels: 43.9 us -> 41.9 us
    pallas_call x1, Pallas kernels: 41.9 us -> 39.9 us  [on_device(): pl.pallas_call(functools.partial(kernel, size, heads, far), out_shape=(ou...]
where the time goes in v5:
time: 42.7 us; the launch traced here: 42.5 us
  Pallas kernels  41.9 us (98%)
  between operations  0.64 us (1%)
    pallas_call x1, Pallas kernels, on_device(): pl.pallas_call(functools.partial(kernel, size, heads, far), out_shape=(ou...  39.9 us
    pallas_call x1, Pallas kernels, on_device(): pl.pallas_call(copy_out, out_shape=(out,) * 4, in_specs=[hbm] * 4, out_sp...  1.98 us

profile of v5, /device:TPU:0, one launch (start us, length us, event | category | flops | bytes accessed | tf_op | source)
XLA Modules:
  0.0 42.5 jit_solution(10947915534397931908)
XLA Ops:
  0.6 39.9 %shard_map.93 = (bf16[256,512]{1,0:T(8,128)(2,1)}, bf16[256,512]{1,0:T(8,128)(2,1)}, bf16[256,512]{1,0:T(8,128)(2,1)}, bf16[256,512]{1,0:T(8,128)(2,1)}) custom-call(s32[4]{0:T(128)} %window_hbm.1, s32[4,4]{1,0:T(4,128)} %offsets_hbm.1, bf16[256,512]{1,0:T(8,128)(2,1)} %q_hbm.1, bf16[256,512]{1,0:T(8,128)(2,1)} %k_hbm.1, bf16[256,512]{1,0:T(8,128)(2,1)} %v_hbm.1, ...), custom_call_target="tpu_custom_call" | custom-call | flops 1610612736 | bytes 2097152 | tf_op jit(solution)/shard_map/pallas_call | solution.py:455
  40.5 2.0 %shard_map.94 = (bf16[256,512]{1,0:T(8,128)(2,1)}, bf16[256,512]{1,0:T(8,128)(2,1)}, bf16[256,512]{1,0:T(8,128)(2,1)}, bf16[256,512]{1,0:T(8,128)(2,1)}) custom-call(bf16[256,512]{1,0:T(8,128)(2,1)} %get-tuple-element.8.refs_0_, bf16[256,512]{1,0:T(8,128)(2,1)} %get-tuple-element.9.refs_1_, bf16[256,512]{1,0:T(8,128)(2,1)} %get-tuple-element.10.refs_2_, ...), custom_call_target="tpu_custom_call" | custom-call | bytes 2097152 | tf_op jit(solution)/shard_map/pallas_call | solution.py:482

commit v6 on v5

--- a/solution.py
+++ b/solution.py
@@ -137,13 +137,13 @@
     def start_own(i):
         loads[i // 2][i % 2].wait()
 
+        @pl.when(even)
+        def _():
+            prev_own(i).start()
+
         @pl.when(has_up)
         def _():
             own_up(i).start()
-
-        @pl.when(even)
-        def _():
-            prev_own(i).start()
 
         for n in range(len(far)):
 
@@ -268,15 +268,15 @@
         def keep(which, near, log, x, factor):
             i = 2 * h + which
             parts = [dot(block(log, p), block(x, p), TN) for p in range(groups)]
+            flip = near.T
+            flip_own = flip * tri_low[1]
+            tg1[h, which] = (dot(flip - flip_own, x, NN) * factor).astype(bf16)
+            send_near(i)
             for n in range(len(far)):
                 tgf[n, h, which] = (scattered(parts, 2 + n) * factor).astype(bf16)
             if len(dists) > 1:
                 tg4[h, which] = (scattered(parts, 1) * factor).astype(bf16)
             send_far(i)
-            flip = near.T
-            flip_own = flip * tri_low[1]
-            tg1[h, which] = (dot(flip - flip_own, x, NN) * factor).astype(bf16)
-            send_near(i)
             hold2[h, which] = scattered(parts, 0) * factor
             acc[h, which] = dot(flip_own, x, NN) * factor
 
@@ -321,13 +321,13 @@
         def _():
             own_up(i).wait_recv()
 
+        @pl.when(odd & (r >= 3))
+        def _():
+            prev_relay(i).start()
+
         @pl.when((r >= 2) & has_up)
         def _():
             relay_up(i).start()
-
-        @pl.when(odd & (r >= 3))
-        def _():
-            prev_relay(i).start()
 
         if i + AHEAD < pieces:
             start_own(i + AHEAD)

time: 42.7 us -> 42.7 us (level)
  no operation moved by 1% of the time
where the time goes in v6:
time: 42.7 us; the launch traced here: 42.5 us
  Pallas kernels  41.9 us (98%)
  between operations  0.64 us (1%)
    pallas_call x1, Pallas kernels, on_device(): pl.pallas_call(functools.partial(kernel, size, heads, far), out_shape=(ou...  39.9 us
    pallas_call x1, Pallas kernels, on_device(): pl.pallas_call(copy_out, out_shape=(out,) * 4, in_specs=[hbm] * 4, out_sp...  1.98 us

profile of v6, /device:TPU:0, one launch (start us, length us, event | category | flops | bytes accessed | tf_op | source)
XLA Modules:
  0.0 42.5 jit_solution(16844453763237032668)
XLA Ops:
  0.6 39.9 %shard_map.93 = (bf16[256,512]{1,0:T(8,128)(2,1)}, bf16[256,512]{1,0:T(8,128)(2,1)}, bf16[256,512]{1,0:T(8,128)(2,1)}, bf16[256,512]{1,0:T(8,128)(2,1)}) custom-call(s32[4]{0:T(128)} %window_hbm.1, s32[4,4]{1,0:T(4,128)} %offsets_hbm.1, bf16[256,512]{1,0:T(8,128)(2,1)} %q_hbm.1, bf16[256,512]{1,0:T(8,128)(2,1)} %k_hbm.1, bf16[256,512]{1,0:T(8,128)(2,1)} %v_hbm.1, ...), custom_call_target="tpu_custom_call" | custom-call | flops 1610612736 | bytes 2097152 | tf_op jit(solution)/shard_map/pallas_call | solution.py:455
  40.6 2.0 %shard_map.94 = (bf16[256,512]{1,0:T(8,128)(2,1)}, bf16[256,512]{1,0:T(8,128)(2,1)}, bf16[256,512]{1,0:T(8,128)(2,1)}, bf16[256,512]{1,0:T(8,128)(2,1)}) custom-call(bf16[256,512]{1,0:T(8,128)(2,1)} %get-tuple-element.8.refs_0_, bf16[256,512]{1,0:T(8,128)(2,1)} %get-tuple-element.9.refs_1_, bf16[256,512]{1,0:T(8,128)(2,1)} %get-tuple-element.10.refs_2_, ...), custom_call_target="tpu_custom_call" | custom-call | bytes 2097152 | tf_op jit(solution)/shard_map/pallas_call | solution.py:482

commit v7 on v6

--- a/solution.py
+++ b/solution.py
@@ -374,13 +374,16 @@
     steps = [compute(h) for h in range(heads)]
     for i in range(AHEAD):
         relay(i)
+    done = 0
     for i in range(pieces):
         next(steps[i // 2])
         if i + AHEAD < pieces:
             relay(i + AHEAD)
-        if i >= LAG:
-            combine(back[i - LAG])
-    for i in back[-LAG:]:
+        due = i - LAG + (i >= pieces - 2)
+        while done <= due:
+            combine(back[done])
+            done += 1
+    for i in back[done:]:
         combine(i)
     for i in back:
         finish(i)

time: 42.7 us -> 43.1 us (level)
  no operation moved by 1% of the time
where the time goes in v7:
time: 43.1 us; the launch traced here: 42.9 us
  Pallas kernels  42.3 us (98%)
  between operations  0.64 us (1%)
    pallas_call x1, Pallas kernels, on_device(): pl.pallas_call(functools.partial(kernel, size, heads, far), out_shape=(ou...  40.3 us
    pallas_call x1, Pallas kernels, on_device(): pl.pallas_call(copy_out, out_shape=(out,) * 4, in_specs=[hbm] * 4, out_sp...  1.98 us

profile of v7, /device:TPU:0, one launch (start us, length us, event | category | flops | bytes accessed | tf_op | source)
XLA Modules:
  0.0 42.9 jit_solution(14646044669927573790)
XLA Ops:
  0.6 40.3 %shard_map.93 = (bf16[256,512]{1,0:T(8,128)(2,1)}, bf16[256,512]{1,0:T(8,128)(2,1)}, bf16[256,512]{1,0:T(8,128)(2,1)}, bf16[256,512]{1,0:T(8,128)(2,1)}) custom-call(s32[4]{0:T(128)} %window_hbm.1, s32[4,4]{1,0:T(4,128)} %offsets_hbm.1, bf16[256,512]{1,0:T(8,128)(2,1)} %q_hbm.1, bf16[256,512]{1,0:T(8,128)(2,1)} %k_hbm.1, bf16[256,512]{1,0:T(8,128)(2,1)} %v_hbm.1, ...), custom_call_target="tpu_custom_call" | custom-call | flops 1610612736 | bytes 2097152 | tf_op jit(solution)/shard_map/pallas_call | solution.py:458
  41.0 2.0 %shard_map.94 = (bf16[256,512]{1,0:T(8,128)(2,1)}, bf16[256,512]{1,0:T(8,128)(2,1)}, bf16[256,512]{1,0:T(8,128)(2,1)}, bf16[256,512]{1,0:T(8,128)(2,1)}) custom-call(bf16[256,512]{1,0:T(8,128)(2,1)} %get-tuple-element.8.refs_0_, bf16[256,512]{1,0:T(8,128)(2,1)} %get-tuple-element.9.refs_1_, bf16[256,512]{1,0:T(8,128)(2,1)} %get-tuple-element.10.refs_2_, ...), custom_call_target="tpu_custom_call" | custom-call | bytes 2097152 | tf_op jit(solution)/shard_map/pallas_call | solution.py:485

commit v8 on v6

--- a/solution.py
+++ b/solution.py
@@ -29,7 +29,7 @@
     window_hbm, offsets_hbm, q_hbm, k_hbm, v_hbm, do_hbm,
     att_hbm, gq_hbm, gk_hbm, gv_hbm,
     staged, window, offsets, q_ref, do_ref, tri_low, own, rx1, rx2, rx4, rxf,
-    tg1, tg4, ts2, tgf, rg1, rg4, rs2, rgf, hold2, acc,
+    tg1, tg4, ts2, tgf, rg1, rg4, rs2, rgd, rgf, hold2, acc,
     send, recv, load, load_small, store,
 ):
     f32, bf16 = jnp.float32, jnp.bfloat16
@@ -38,11 +38,18 @@
     odd = lax.rem(r, 2) == 1
     even = jnp.logical_not(odd)
     has_up = r + 2 < size
+    direct = lax.rem(r // 2, 2) == 0
+    passes = direct & (r >= 2) & has_up
+    has_up4 = direct & (r + 4 < size)
+    has_down4 = direct & (r >= 4)
+    via = jnp.logical_not(direct) & (r >= 4)
     scale = HEAD ** -0.5
     mate = r + 1 - 2 * lax.rem(r, 2)
 
     K_OWN, K_REL, K_PRV, K_G4, K_S2, K_G1, K_FAR = 0, 1, 2, 3, 4, 5, 6
     K_GFAR = K_FAR + len(far)
+    K_DIR = K_GFAR + len(far)
+    K_GDIR = K_DIR + 1
 
     def copy(kind, h, src, dst, to):
         return pltpu.make_async_remote_copy(
@@ -58,6 +65,12 @@
 
     def relay_up(i):
         return copy(K_REL, i, piece(rx2, i), piece(rx4, i), r + 2)
+
+    def direct_up(i):
+        return copy(K_DIR, i, piece(own, i), piece(rx4, i), r + 4)
+
+    def direct_down(i):
+        return copy(K_GDIR, i, piece(tg4, i), piece(rgd, i), r - 4)
 
     def prev_own(i):
         return copy(K_PRV, i, piece(own, i), piece(rx1, i), mate)
@@ -110,7 +123,7 @@
     barrier = pltpu.get_barrier_semaphore()
     pl.semaphore_signal(barrier, inc=1, device_id={"ctx": mate}, device_id_type=MESH)
     count = 1
-    for d in (2,) + far:
+    for d in (2, 4) + far:
         for to, ok in ((r + d, r + d < size), (r - d, r >= d)):
             count = count + ok.astype(jnp.int32)
 
@@ -144,6 +157,10 @@
         @pl.when(has_up)
         def _():
             own_up(i).start()
+
+        @pl.when(has_up4)
+        def _():
+            direct_up(i).start()
 
         for n in range(len(far)):
 
@@ -189,9 +206,13 @@
         return x[p * BLOCK:(p + 1) * BLOCK]
 
     def send_far(i):
-        @pl.when(r >= 4)
+        @pl.when(via)
         def _():
             g4_down(i).start()
+
+        @pl.when(has_down4)
+        def _():
+            direct_down(i).start()
 
         for n in range(len(far)):
 
@@ -301,7 +322,7 @@
     def combine(i):
         h, w = i // 2, i % 2
 
-        @pl.when((r >= 2) & has_up)
+        @pl.when(passes)
         def _():
             g4_down(i).wait_recv()
             hold2[h, w] = hold2[h, w] + rg4[h, w].astype(f32)
@@ -325,7 +346,7 @@
         def _():
             prev_relay(i).start()
 
-        @pl.when((r >= 2) & has_up)
+        @pl.when(passes)
         def _():
             relay_up(i).start()
 
@@ -337,9 +358,13 @@
         def _():
             prev_own(i).wait_recv()
 
-        @pl.when(r >= 4)
+        @pl.when(via)
         def _():
             relay_up(i).wait_recv()
+
+        @pl.when(has_down4)
+        def _():
+            direct_up(i).wait_recv()
 
         for n in range(len(far)):
 
@@ -361,6 +386,11 @@
             def _(n=n):
                 gfar_down(n, i).wait_recv()
                 acc[h, w] = acc[h, w] + rgf[n, h, w].astype(f32)
+
+        @pl.when(has_up4)
+        def _():
+            direct_down(i).wait_recv()
+            acc[h, w] = acc[h, w] + rgd[h, w].astype(f32)
 
         @pl.when(has_up)
         def _():
@@ -391,17 +421,25 @@
         def _(i=i):
             own_up(i).wait_send()
 
-        @pl.when((r >= 2) & has_up)
+        @pl.when(passes)
         def _(i=i):
             relay_up(i).wait_send()
 
+        @pl.when(has_up4)
+        def _(i=i):
+            direct_up(i).wait_send()
+
         @pl.when(even | (r >= 3))
         def _(i=i):
             prev_own(i).wait_send()
 
-        @pl.when(r >= 4)
+        @pl.when(via)
         def _(i=i):
             g4_down(i).wait_send()
+
+        @pl.when(has_down4)
+        def _(i=i):
+            direct_down(i).wait_send()
 
         @pl.when(r >= 2)
         def _(i=i):
@@ -445,7 +483,7 @@
     heads = feat // HEAD
     far = tuple(2 ** (j + 1) for j in range(2, LEVELS) if 2 ** (j + 1) < size)
     nf = max(len(far), 1)
-    kinds = 6 + 2 * len(far)
+    kinds = 8 + 2 * len(far)
     hbm = pl.BlockSpec(memory_space=pltpu.HBM)
     pack = (heads, 2, rows, HEAD)
     small = pltpu.VMEM(pack, jnp.bfloat16)
@@ -465,7 +503,7 @@
             pltpu.VMEM((heads, rows, HEAD), jnp.bfloat16),
             pltpu.VMEM((2, rows, rows), jnp.bfloat16),
         ]
-        + [small] * 4 + [more] + [small] * 3 + [more] + [small] * 3 + [more]
+        + [small] * 4 + [more] + [small] * 3 + [more] + [small] * 4 + [more]
         + [wide] * 2
         + [pltpu.SemaphoreType.DMA((kinds, 2 * heads)), pltpu.SemaphoreType.DMA((kinds, 2 * heads))]
         + [pltpu.SemaphoreType.DMA((heads, 4)), pltpu.SemaphoreType.DMA((2,))]

time: 42.7 us -> 44.9 us (1.052)
  Pallas kernels: 41.9 us -> 44.1 us
    pallas_call x1, Pallas kernels: 39.9 us -> 42.1 us  [on_device(): pl.pallas_call(functools.partial(kernel, size, heads, far), out_shape=(ou...]
where the time goes in v8:
time: 44.9 us; the launch traced here: 44.7 us
  Pallas kernels  44.1 us (98%)
  between operations  0.64 us (1%)
    pallas_call x1, Pallas kernels, on_device(): pl.pallas_call(functools.partial(kernel, size, heads, far), out_shape=(ou...  42.1 us
    pallas_call x1, Pallas kernels, on_device(): pl.pallas_call(copy_out, out_shape=(out,) * 4, in_specs=[hbm] * 4, out_sp...  1.98 us

profile of v8, /device:TPU:0, one launch (start us, length us, event | category | flops | bytes accessed | tf_op | source)
XLA Modules:
  0.0 44.7 jit_solution(8394419247745437169)
XLA Ops:
  0.6 42.1 %shard_map.93 = (bf16[256,512]{1,0:T(8,128)(2,1)}, bf16[256,512]{1,0:T(8,128)(2,1)}, bf16[256,512]{1,0:T(8,128)(2,1)}, bf16[256,512]{1,0:T(8,128)(2,1)}) custom-call(s32[4]{0:T(128)} %window_hbm.1, s32[4,4]{1,0:T(4,128)} %offsets_hbm.1, bf16[256,512]{1,0:T(8,128)(2,1)} %q_hbm.1, bf16[256,512]{1,0:T(8,128)(2,1)} %k_hbm.1, bf16[256,512]{1,0:T(8,128)(2,1)} %v_hbm.1, ...), custom_call_target="tpu_custom_call" | custom-call | flops 1610612736 | bytes 2097152 | tf_op jit(solution)/shard_map/pallas_call | solution.py:493
  42.7 2.0 %shard_map.94 = (bf16[256,512]{1,0:T(8,128)(2,1)}, bf16[256,512]{1,0:T(8,128)(2,1)}, bf16[256,512]{1,0:T(8,128)(2,1)}, bf16[256,512]{1,0:T(8,128)(2,1)}) custom-call(bf16[256,512]{1,0:T(8,128)(2,1)} %get-tuple-element.8.refs_0_, bf16[256,512]{1,0:T(8,128)(2,1)} %get-tuple-element.9.refs_1_, bf16[256,512]{1,0:T(8,128)(2,1)} %get-tuple-element.10.refs_2_, ...), custom_call_target="tpu_custom_call" | custom-call | bytes 2097152 | tf_op jit(solution)/shard_map/pallas_call | solution.py:520

commit v9 on v6

--- a/solution.py
+++ b/solution.py
@@ -13,7 +13,7 @@
 HEAD = 128
 NEG = -1e30
 AHEAD = 2
-LAG = 2
+LAG = 3
 MESH = pl.DeviceIdType.MESH
 NT = (((1,), (1,)), ((), ()))
 TN = (((0,), (0,)), ((), ()))

time: 42.7 us -> 43.3 us (1.014)
  Pallas kernels: 41.9 us -> 42.5 us
    pallas_call x1, Pallas kernels: 39.9 us -> 40.5 us  [on_device(): pl.pallas_call(functools.partial(kernel, size, heads, far), out_shape=(ou...]
where the time goes in v9:
time: 43.3 us; the launch traced here: 43.2 us
  Pallas kernels  42.5 us (98%)
  between operations  0.64 us (1%)
    pallas_call x1, Pallas kernels, on_device(): pl.pallas_call(functools.partial(kernel, size, heads, far), out_shape=(ou...  40.5 us
    pallas_call x1, Pallas kernels, on_device(): pl.pallas_call(copy_out, out_shape=(out,) * 4, in_specs=[hbm] * 4, out_sp...  1.98 us

profile of v9, /device:TPU:0, one launch (start us, length us, event | category | flops | bytes accessed | tf_op | source)
XLA Modules:
  0.0 43.2 jit_solution(3511128727029281657)
XLA Ops:
  0.6 40.5 %shard_map.93 = (bf16[256,512]{1,0:T(8,128)(2,1)}, bf16[256,512]{1,0:T(8,128)(2,1)}, bf16[256,512]{1,0:T(8,128)(2,1)}, bf16[256,512]{1,0:T(8,128)(2,1)}) custom-call(s32[4]{0:T(128)} %window_hbm.1, s32[4,4]{1,0:T(4,128)} %offsets_hbm.1, bf16[256,512]{1,0:T(8,128)(2,1)} %q_hbm.1, bf16[256,512]{1,0:T(8,128)(2,1)} %k_hbm.1, bf16[256,512]{1,0:T(8,128)(2,1)} %v_hbm.1, ...), custom_call_target="tpu_custom_call" | custom-call | flops 1610612736 | bytes 2097152 | tf_op jit(solution)/shard_map/pallas_call | solution.py:455
  41.2 2.0 %shard_map.94 = (bf16[256,512]{1,0:T(8,128)(2,1)}, bf16[256,512]{1,0:T(8,128)(2,1)}, bf16[256,512]{1,0:T(8,128)(2,1)}, bf16[256,512]{1,0:T(8,128)(2,1)}) custom-call(bf16[256,512]{1,0:T(8,128)(2,1)} %get-tuple-element.8.refs_0_, bf16[256,512]{1,0:T(8,128)(2,1)} %get-tuple-element.9.refs_1_, bf16[256,512]{1,0:T(8,128)(2,1)} %get-tuple-element.10.refs_2_, ...), custom_call_target="tpu_custom_call" | custom-call | bytes 2097152 | tf_op jit(solution)/shard_map/pallas_call | solution.py:482
